TPU v7x, 512 devices: a whole 4x4x16 slice. The times are simulated.
512 devices in a mesh: gx: 16 (over z), gy: 32 (over y, x, core).
Axes of the slice: x: 4, y: 4, z: 16, core: 2. Of those that a mesh axis runs over, the one named last changes fastest.
Arguments:
- field_now: float32 [512, 8, 4096], P('gx', None, 'gy'), may hold values from -6 to 6
- base_cond: float32 [512, 8, 4096], P('gx', None, 'gy'), may hold values from 1.4 to 2.8
- spacing: float32 [512], P('gx'), may hold values from 0.45 to 0.65
- source: float32 [512, 8, 4096], P('gx', None, 'gy'), may hold values from -6 to 7.5
Outputs:
- field_half: float32 [512, 8, 4096], P('gx', None, 'gy')
- face_flux: float32 [512, 8, 4096], P('gx', None, 'gy')
All inputs are finite; a program needn't handle non-finite values.
Results may differ from a plain program's by a relative error of at most 0.0019.
Values sent between devices are 32-bit elements; how exact they have to be, the bound alone decides.
A program may use at most 64 MiB of HBM per device.

v0:
```python
import jax
import jax.numpy as jnp
from jax import lax
from jax.sharding import PartitionSpec as P

y_weight = 0.15
z_weight = 0.1
source_gain = 1.0


def padded(value, sides, width):
    for axis, dim in sides:
        size, length = (lax.axis_size(axis), value.shape[dim])
        up = [(i, (i + 1) % size) for i in range(size - 1)]
        down = [(j, i) for i, j in up]
        last = lax.slice_in_dim(value, length - width, length, axis=dim)
        initial = lax.slice_in_dim(value, 0, width, axis=dim)
        before = lax.ppermute(last, axis, up)
        after = lax.ppermute(initial, axis, down)
        value = jnp.concatenate([before, value, after], axis=dim)
    return value


def from_behind(block, axis, distance):
    devices = range(lax.axis_size(axis))
    route = [(i - distance, i) for i in devices if i - distance in devices]
    return lax.ppermute(block, axis, route)


def conduct(field, base_cond):
    square = field * field
    return base_cond * (1.0 + square / (1.0 + square))


def harmonic(first, second):
    return 2.0 * first * second / (first + second)


def combine(own, below, above, extras):
    sub_diag, main_diag, sup_diag, right = own
    low_main = jnp.where(below[1] == 0, 1.0, below[1])
    high_main = jnp.where(above[1] == 0, 1.0, above[1])
    left_ratio = sub_diag / low_main
    right_ratio = sup_diag / high_main
    rows = (
        -left_ratio * below[0],
        main_diag - left_ratio * below[2] - right_ratio * above[0],
        -right_ratio * above[2],
        right - left_ratio * below[3] - right_ratio * above[3],
    )
    more = tuple(
        (
            value - left_ratio * value_low - right_ratio * value_high
            for value, value_low, value_high in extras
        )
    )
    return (rows, more)


def reduce_level(rows, extras, stride):

    def below(value):
        return jnp.concatenate([jnp.zeros_like(value[:stride]), value[:-stride]], 0)

    def above(value):
        return jnp.concatenate([value[stride:], jnp.zeros_like(value[-stride:])], 0)

    pieces = tuple(((value, below(value), above(value)) for value in extras))
    return combine(
        rows,
        tuple((below(value) for value in rows)),
        tuple((above(value) for value in rows)),
        pieces,
    )


def implicit_solve(cond, spacing, right, stiff):
    width = cond.shape[0]
    cell = jnp.broadcast_to(spacing[:, None, None], cond.shape)
    rimmed = padded(jnp.stack([cond, cell], axis=1), (("gx", 0),), 1)
    cond_prev = jnp.where(rimmed[:-2, 0] == 0, cond, rimmed[:-2, 0])
    cell_prev = jnp.where(rimmed[:-2, 1] == 0, cell, rimmed[:-2, 1])
    cond_next = jnp.where(rimmed[2:, 0] == 0, cond, rimmed[2:, 0])
    cell_next = jnp.where(rimmed[2:, 1] == 0, cell, rimmed[2:, 1])
    w_up = stiff * harmonic(cond, cond_next) / (0.5 * (cell + cell_next))
    w_down = stiff * harmonic(cond, cond_prev) / (0.5 * (cell + cell_prev))
    lower = -w_down
    middle = cell + w_up + w_down
    upper = -w_up
    index = lax.broadcasted_iota(jnp.int32, cond.shape, 0)
    edge = (index == 0) | (index == width - 1)
    alpha = jnp.where(index == 1, lower, 0.0)
    gamma = jnp.where(index == width - 2, upper, 0.0)
    rows = (
        jnp.where(edge | (index == 1), 0.0, lower),
        jnp.where(edge, 1.0, middle),
        jnp.where(edge | (index == width - 2), 0.0, upper),
        jnp.where(edge, 0.0, right),
    )
    extras = (alpha, gamma)
    stride = 1
    while stride < width:
        rows, extras = reduce_level(rows, extras, stride)
        stride = stride * 2
    inner_main, inner_right = (rows[1], rows[3])
    alpha, gamma = extras
    first_sub = lower[0]
    first_main = middle[0] - upper[0] * alpha[1] / inner_main[1]
    first_sup = -upper[0] * gamma[1] / inner_main[1]
    first_right = right[0] - upper[0] * inner_right[1] / inner_main[1]
    last_sub = -lower[width - 1] * alpha[width - 2] / inner_main[width - 2]
    last_main = middle[width - 1] - lower[width - 1] * gamma[width - 2] / inner_main[width - 2]
    last_sup = upper[width - 1]
    last_right = (
        right[width - 1] - lower[width - 1] * inner_right[width - 2] / inner_main[width - 2]
    )
    first_rows = (first_sub, first_main, first_sup, first_right)
    next_rows = from_behind((first_sub, first_main, first_sup, first_right), "gx", -1)
    reduced, _ = combine((last_sub, last_main, last_sup, last_right), first_rows, next_rows, ())
    parts = lax.axis_size("gx")
    stride = 1
    while stride < parts:
        lower_part = from_behind((reduced[0], reduced[1], reduced[2], reduced[3]), "gx", stride)
        upper_part = from_behind((reduced[0], reduced[1], reduced[2], reduced[3]), "gx", -stride)
        reduced, _ = combine(reduced, lower_part, upper_part, ())
        stride = stride * 2
    last_value = reduced[3] / reduced[1]
    prev_last = from_behind(last_value, "gx", 1)
    first_value = (first_right - first_sub * prev_last - first_sup * last_value) / first_main
    inner = (inner_right - alpha * first_value[None] - gamma * last_value[None]) / inner_main
    solved = jnp.where(
        index == 0, first_value[None], jnp.where(index == width - 1, last_value[None], inner)
    )
    return (solved, w_up)


def per_device(field_now, base_cond, spacing, source):
    width = field_now.shape[0]
    stiff = 4.0 * width * width
    cond_start = conduct(field_now, base_cond)
    rimmed = padded(jnp.stack([field_now, cond_start], axis=1), (("gy", 3),), 1)
    field_ext = rimmed[:, 0]
    cond_ext = rimmed[:, 1]
    dy = y_weight * harmonic(cond_start, cond_ext[:, :, 2:]) * (field_ext[:, :, 2:] - field_now)
    dy = dy + y_weight * harmonic(cond_start, cond_ext[:, :, :-2]) * (
        field_ext[:, :, :-2] - field_now
    )
    face_z = (
        z_weight
        * harmonic(cond_start[:, :-1], cond_start[:, 1:])
        * (field_now[:, 1:] - field_now[:, :-1])
    )
    zero_face = jnp.zeros_like(face_z[:, :1])
    dz = jnp.concatenate([face_z, zero_face], 1) - jnp.concatenate([zero_face, face_z], 1)
    cell = spacing[:, None, None]
    right = cell * (field_now + dy + dz + source_gain * source)
    field_first, _ = implicit_solve(cond_start, spacing, right, stiff)
    cond_next = conduct(0.5 * (field_now + field_first), base_cond)
    field_half, w_up = implicit_solve(cond_next, spacing, right, stiff)
    following = from_behind(field_half[:1], "gx", -1)
    ahead = jnp.concatenate([field_half[1:], following], 0)
    face_flux = w_up * (field_half - ahead) / width
    return (field_half, face_flux)


def solution(mesh):
    placed = (P("gx", None, "gy"), P("gx", None, "gy"), P("gx"), P("gx", None, "gy"))
    return jax.shard_map(
        per_device,
        mesh=mesh,
        in_specs=placed,
        out_specs=(P("gx", None, "gy"), P("gx", None, "gy")),
        check_vma=False,
    )
```

profile of v0, /device:TPU:24, one launch (start us, length us, event | category | flops | bytes accessed | tf_op | source)
XLA Modules:
  0.0 399.6 jit_solution(8285762229421237174)
XLA Ops:
  3.8 4.5 %collective-permute-start.3 = (f32[1,2,8,128]{3,2,0,1:T(8,128)S(1)}, f32[1,2,8,128]{3,2,0,1:T(8,128)S(1)}, u32[]{:S(2)}, u32[]{:S(2)}) collective-permute-start(f32[1,2,8,128]{3,2,0,1:T(8,128)S(1)} %get-tuple-element.161), channel_id=1, source_target_pairs={{0,32},{32,64},{64,96},{96,128},{128,160},{160,192},{192,224},{224... | collective-permute-start | bytes 24584 | tf_op jit(solution)/shard_map/ppermute | solution.py:18
  8.5 1.9 collective-permute-start
  10.5 5.8 %collective-permute-start.1 = (f32[32,2,8,1]{3,2,0,1:T(8,128)S(1)}, f32[32,2,8,1]{3,2,0,1:T(8,128)S(1)}, u32[]{:S(2)}, u32[]{:S(2)}) collective-permute-start(f32[32,2,8,1]{3,2,0,1:T(8,128)S(1)} %get-tuple-element.157), channel_id=1, source_target_pairs={{1,0},{2,1},{3,2},{4,3},{5,4},{6,5},{7,6},{8,7},{9,8},{10,9},{11,1... | collective-permute-start | bytes 6152 | tf_op jit(solution)/shard_map/ppermute | solution.py:19
  16.3 2.0 collective-permute-done
  29.0 1.9 collective-permute-done.5
  31.0 1.9 collective-permute-done.6
  34.2 4.5 %collective-permute-start.7 = (f32[8,128]{1,0:T(8,128)S(1)}, f32[8,128]{1,0:T(8,128)S(1)}, u32[]{:S(2)}, u32[]{:S(2)}) collective-permute-start(f32[8,128]{1,0:T(8,128)S(1)} %get-tuple-element.55), channel_id=1, source_target_pairs={{0,32},{32,64},{64,96},{96,128},{128,160},{160,192},{192,224},{224... | collective-permute-start | bytes 12296 | tf_op jit(solution)/shard_map/ppermute | solution.py:27
  41.3 6.1 %collective-permute-start.8 = (f32[8,128]{1,0:T(8,128)S(1)}, f32[8,128]{1,0:T(8,128)S(1)}, u32[]{:S(2)}, u32[]{:S(2)}) collective-permute-start(f32[8,128]{1,0:T(8,128)S(1)} %get-tuple-element.53), channel_id=1, source_target_pairs={{0,32},{32,64},{64,96},{96,128},{128,160},{160,192},{192,224},{224... | collective-permute-start | bytes 12296 | tf_op jit(solution)/shard_map/ppermute | solution.py:27
  48.8 5.1 %collective-permute-start.13 = (f32[8,128]{1,0:T(8,128)S(1)}, f32[8,128]{1,0:T(8,128)S(1)}, u32[]{:S(2)}, u32[]{:S(2)}) collective-permute-start(f32[8,128]{1,0:T(8,128)S(1)} %get-tuple-element.51), channel_id=1, source_target_pairs={{0,32},{32,64},{64,96},{96,128},{128,160},{160,192},{192,224},{224... | collective-permute-start | bytes 12296 | tf_op jit(solution)/shard_map/ppermute | solution.py:27
  55.2 5.8 %collective-permute-start.12 = (f32[8,128]{1,0:T(8,128)S(1)}, f32[8,128]{1,0:T(8,128)S(1)}, u32[]{:S(2)}, u32[]{:S(2)}) collective-permute-start(f32[8,128]{1,0:T(8,128)S(1)} %get-tuple-element.52), channel_id=1, source_target_pairs={{0,32},{32,64},{64,96},{96,128},{128,160},{160,192},{192,224},{224... | collective-permute-start | bytes 12296 | tf_op jit(solution)/shard_map/ppermute | solution.py:27
  62.3 8.7 %collective-permute-start.16 = (f32[8,128]{1,0:T(8,128)S(1)}, f32[8,128]{1,0:T(8,128)S(1)}, u32[]{:S(2)}, u32[]{:S(2)}) collective-permute-start(f32[8,128]{1,0:T(8,128)S(1)} %get-tuple-element.50), channel_id=1, source_target_pairs={{0,64},{32,96},{64,128},{96,160},{128,192},{160,224},{192,256},{22... | collective-permute-start | bytes 12296 | tf_op jit(solution)/shard_map/ppermute | solution.py:27
  72.3 8.4 %collective-permute-start.15 = (f32[8,128]{1,0:T(8,128)S(1)}, f32[8,128]{1,0:T(8,128)S(1)}, u32[]{:S(2)}, u32[]{:S(2)}) collective-permute-start(f32[8,128]{1,0:T(8,128)S(1)} %multiply_subtract_fusion.50), channel_id=1, source_target_pairs={{0,64},{32,96},{64,128},{96,160},{128,192},{160,224},{192,256},{22... | collective-permute-start | bytes 12296 | tf_op jit(solution)/shard_map/ppermute | solution.py:27
  82.1 6.3 %collective-permute-done.18 = f32[8,128]{1,0:T(8,128)S(1)} collective-permute-done((f32[8,128]{1,0:T(8,128)S(1)}, f32[8,128]{1,0:T(8,128)S(1)}, u32[]{:S(2)}, u32[]{:S(2)}) %collective-permute-start.18) | collective-permute-done | bytes 4128 | tf_op jit(solution)/shard_map/ppermute | solution.py:27
  88.4 6.2 %collective-permute-start.21 = (f32[8,128]{1,0:T(8,128)S(1)}, f32[8,128]{1,0:T(8,128)S(1)}, u32[]{:S(2)}, u32[]{:S(2)}) collective-permute-start(f32[8,128]{1,0:T(8,128)S(1)} %get-tuple-element.48), channel_id=1, source_target_pairs={{0,64},{32,96},{64,128},{96,160},{128,192},{160,224},{192,256},{22... | collective-permute-start | bytes 12296 | tf_op jit(solution)/shard_map/ppermute | solution.py:27
  95.9 6.2 %collective-permute-start.20 = (f32[8,128]{1,0:T(8,128)S(1)}, f32[8,128]{1,0:T(8,128)S(1)}, u32[]{:S(2)}, u32[]{:S(2)}) collective-permute-start(f32[8,128]{1,0:T(8,128)S(1)} %get-tuple-element.49), channel_id=1, source_target_pairs={{0,64},{32,96},{64,128},{96,160},{128,192},{160,224},{192,256},{22... | collective-permute-start | bytes 12296 | tf_op jit(solution)/shard_map/ppermute | solution.py:27
  103.4 10.2 %collective-permute-start.24 = (f32[8,128]{1,0:T(8,128)S(1)}, f32[8,128]{1,0:T(8,128)S(1)}, u32[]{:S(2)}, u32[]{:S(2)}) collective-permute-start(f32[8,128]{1,0:T(8,128)S(1)} %get-tuple-element.47), channel_id=1, source_target_pairs={{0,128},{32,160},{64,192},{96,224},{128,256},{160,288},{192,320},{... | collective-permute-start | bytes 12296 | tf_op jit(solution)/shard_map/ppermute | solution.py:27
  114.9 8.5 %collective-permute-start.23 = (f32[8,128]{1,0:T(8,128)S(1)}, f32[8,128]{1,0:T(8,128)S(1)}, u32[]{:S(2)}, u32[]{:S(2)}) collective-permute-start(f32[8,128]{1,0:T(8,128)S(1)} %multiply_subtract_fusion.48), channel_id=1, source_target_pairs={{0,128},{32,160},{64,192},{96,224},{128,256},{160,288},{192,320},{... | collective-permute-start | bytes 12296 | tf_op jit(solution)/shard_map/ppermute | solution.py:27
  124.7 8.1 %collective-permute-done.26 = f32[8,128]{1,0:T(8,128)S(1)} collective-permute-done((f32[8,128]{1,0:T(8,128)S(1)}, f32[8,128]{1,0:T(8,128)S(1)}, u32[]{:S(2)}, u32[]{:S(2)}) %collective-permute-start.26) | collective-permute-done | bytes 4128 | tf_op jit(solution)/shard_map/ppermute | solution.py:27
  132.8 7.2 %collective-permute-start.28 = (f32[8,128]{1,0:T(8,128)S(1)}, f32[8,128]{1,0:T(8,128)S(1)}, u32[]{:S(2)}, u32[]{:S(2)}) collective-permute-start(f32[8,128]{1,0:T(8,128)S(1)} %get-tuple-element.46), channel_id=1, source_target_pairs={{0,128},{32,160},{64,192},{96,224},{128,256},{160,288},{192,320},{... | collective-permute-start | bytes 12296 | tf_op jit(solution)/shard_map/ppermute | solution.py:27
  140.0 5.5 %collective-permute-start.29 = (f32[8,128]{1,0:T(8,128)S(1)}, f32[8,128]{1,0:T(8,128)S(1)}, u32[]{:S(2)}, u32[]{:S(2)}) collective-permute-start(f32[8,128]{1,0:T(8,128)S(1)} %get-tuple-element.45), channel_id=1, source_target_pairs={{0,128},{32,160},{64,192},{96,224},{128,256},{160,288},{192,320},{... | collective-permute-start | bytes 12296 | tf_op jit(solution)/shard_map/ppermute | solution.py:27
  148.1 14.4 %collective-permute-start.32 = (f32[8,128]{1,0:T(8,128)S(1)}, f32[8,128]{1,0:T(8,128)S(1)}, u32[]{:S(2)}, u32[]{:S(2)}) collective-permute-start(f32[8,128]{1,0:T(8,128)S(1)} %get-tuple-element.44), channel_id=1, source_target_pairs={{0,256},{32,288},{64,320},{96,352},{128,384},{160,416},{192,448},{... | collective-permute-start | bytes 12296 | tf_op jit(solution)/shard_map/ppermute | solution.py:27
  163.9 13.3 %collective-permute-start.31 = (f32[8,128]{1,0:T(8,128)S(1)}, f32[8,128]{1,0:T(8,128)S(1)}, u32[]{:S(2)}, u32[]{:S(2)}) collective-permute-start(f32[8,128]{1,0:T(8,128)S(1)} %get-tuple-element.286), channel_id=1, source_target_pairs={{0,256},{32,288},{64,320},{96,352},{128,384},{160,416},{192,448},{... | collective-permute-start | bytes 12296 | tf_op jit(solution)/shard_map/ppermute | solution.py:27
  178.5 13.3 %collective-permute-start.36 = (f32[8,128]{1,0:T(8,128)S(1)}, f32[8,128]{1,0:T(8,128)S(1)}, u32[]{:S(2)}, u32[]{:S(2)}) collective-permute-start(f32[8,128]{1,0:T(8,128)S(1)} %get-tuple-element.285), channel_id=1, source_target_pairs={{0,256},{32,288},{64,320},{96,352},{128,384},{160,416},{192,448},{... | collective-permute-start | bytes 12296 | tf_op jit(solution)/shard_map/ppermute | solution.py:27
  193.1 12.9 %collective-permute-done.37 = f32[8,128]{1,0:T(8,128)S(1)} collective-permute-done((f32[8,128]{1,0:T(8,128)S(1)}, f32[8,128]{1,0:T(8,128)S(1)}, u32[]{:S(2)}, u32[]{:S(2)}) %collective-permute-start.37) | collective-permute-done | bytes 4128 | tf_op jit(solution)/shard_map/ppermute | solution.py:27
  210.1 4.8 %collective-permute-start.40 = (f32[1,2,8,128]{3,2,0,1:T(8,128)S(1)}, f32[1,2,8,128]{3,2,0,1:T(8,128)S(1)}, u32[]{:S(2)}, u32[]{:S(2)}) collective-permute-start(f32[1,2,8,128]{3,2,0,1:T(8,128)S(1)} %get-tuple-element.127), channel_id=1, source_target_pairs={{0,32},{32,64},{64,96},{96,128},{128,160},{160,192},{192,224},{224... | collective-permute-start | bytes 24584 | tf_op jit(solution)/shard_map/ppermute | solution.py:18
  222.2 1.9 collective-permute-done.41
  224.0 1.9 collective-permute-done.42
  226.0 1.9 collective-permute-done.43
  227.9 3.9 collective-permute-start.44
  234.4 5.2 %collective-permute-start.45 = (f32[8,128]{1,0:T(8,128)S(1)}, f32[8,128]{1,0:T(8,128)S(1)}, u32[]{:S(2)}, u32[]{:S(2)}) collective-permute-start(f32[8,128]{1,0:T(8,128)S(1)} %get-tuple-element.11), channel_id=1, source_target_pairs={{0,32},{32,64},{64,96},{96,128},{128,160},{160,192},{192,224},{224... | collective-permute-start | bytes 12296 | tf_op jit(solution)/shard_map/ppermute | solution.py:27
  241.0 5.4 %collective-permute-done.48 = f32[8,128]{1,0:T(8,128)S(1)} collective-permute-done((f32[8,128]{1,0:T(8,128)S(1)}, f32[8,128]{1,0:T(8,128)S(1)}, u32[]{:S(2)}, u32[]{:S(2)}) %collective-permute-start.48) | collective-permute-done | bytes 4128 | tf_op jit(solution)/shard_map/ppermute | solution.py:27
  246.3 3.9 collective-permute-start.50
  251.6 5.8 %collective-permute-start.49 = (f32[8,128]{1,0:T(8,128)S(1)}, f32[8,128]{1,0:T(8,128)S(1)}, u32[]{:S(2)}, u32[]{:S(2)}) collective-permute-start(f32[8,128]{1,0:T(8,128)S(1)} %get-tuple-element.10), channel_id=1, source_target_pairs={{0,32},{32,64},{64,96},{96,128},{128,160},{160,192},{192,224},{224... | collective-permute-start | bytes 12296 | tf_op jit(solution)/shard_map/ppermute | solution.py:27
  258.6 7.2 %collective-permute-start.53 = (f32[8,128]{1,0:T(8,128)S(1)}, f32[8,128]{1,0:T(8,128)S(1)}, u32[]{:S(2)}, u32[]{:S(2)}) collective-permute-start(f32[8,128]{1,0:T(8,128)S(1)} %get-tuple-element.8), channel_id=1, source_target_pairs={{0,64},{32,96},{64,128},{96,160},{128,192},{160,224},{192,256},{22... | collective-permute-start | bytes 12296 | tf_op jit(solution)/shard_map/ppermute | solution.py:27
  267.2 7.2 %collective-permute-start.52 = (f32[8,128]{1,0:T(8,128)S(1)}, f32[8,128]{1,0:T(8,128)S(1)}, u32[]{:S(2)}, u32[]{:S(2)}) collective-permute-start(f32[8,128]{1,0:T(8,128)S(1)} %multiply_subtract_fusion.44), channel_id=1, source_target_pairs={{0,64},{32,96},{64,128},{96,160},{128,192},{160,224},{192,256},{22... | collective-permute-start | bytes 12296 | tf_op jit(solution)/shard_map/ppermute | solution.py:27
  275.8 6.3 %collective-permute-done.55 = f32[8,128]{1,0:T(8,128)S(1)} collective-permute-done((f32[8,128]{1,0:T(8,128)S(1)}, f32[8,128]{1,0:T(8,128)S(1)}, u32[]{:S(2)}, u32[]{:S(2)}) %collective-permute-start.55) | collective-permute-done | bytes 4128 | tf_op jit(solution)/shard_map/ppermute | solution.py:27
  282.1 6.0 %collective-permute-start.58 = (f32[8,128]{1,0:T(8,128)S(1)}, f32[8,128]{1,0:T(8,128)S(1)}, u32[]{:S(2)}, u32[]{:S(2)}) collective-permute-start(f32[8,128]{1,0:T(8,128)S(1)} %get-tuple-element.6), channel_id=1, source_target_pairs={{0,64},{32,96},{64,128},{96,160},{128,192},{160,224},{192,256},{22... | collective-permute-start | bytes 12296 | tf_op jit(solution)/shard_map/ppermute | solution.py:27
  289.4 5.4 %collective-permute-start.57 = (f32[8,128]{1,0:T(8,128)S(1)}, f32[8,128]{1,0:T(8,128)S(1)}, u32[]{:S(2)}, u32[]{:S(2)}) collective-permute-start(f32[8,128]{1,0:T(8,128)S(1)} %get-tuple-element.7), channel_id=1, source_target_pairs={{0,64},{32,96},{64,128},{96,160},{128,192},{160,224},{192,256},{22... | collective-permute-start | bytes 12296 | tf_op jit(solution)/shard_map/ppermute | solution.py:27
  296.1 7.3 %collective-permute-start.61 = (f32[8,128]{1,0:T(8,128)S(1)}, f32[8,128]{1,0:T(8,128)S(1)}, u32[]{:S(2)}, u32[]{:S(2)}) collective-permute-start(f32[8,128]{1,0:T(8,128)S(1)} %get-tuple-element.5), channel_id=1, source_target_pairs={{0,128},{32,160},{64,192},{96,224},{128,256},{160,288},{192,320},{... | collective-permute-start | bytes 12296 | tf_op jit(solution)/shard_map/ppermute | solution.py:27
  304.8 8.5 %collective-permute-start.60 = (f32[8,128]{1,0:T(8,128)S(1)}, f32[8,128]{1,0:T(8,128)S(1)}, u32[]{:S(2)}, u32[]{:S(2)}) collective-permute-start(f32[8,128]{1,0:T(8,128)S(1)} %multiply_subtract_fusion.42), channel_id=1, source_target_pairs={{0,128},{32,160},{64,192},{96,224},{128,256},{160,288},{192,320},{... | collective-permute-start | bytes 12296 | tf_op jit(solution)/shard_map/ppermute | solution.py:27
  314.6 8.1 %collective-permute-done.63 = f32[8,128]{1,0:T(8,128)S(1)} collective-permute-done((f32[8,128]{1,0:T(8,128)S(1)}, f32[8,128]{1,0:T(8,128)S(1)}, u32[]{:S(2)}, u32[]{:S(2)}) %collective-permute-start.63) | collective-permute-done | bytes 4128 | tf_op jit(solution)/shard_map/ppermute | solution.py:27
  322.7 5.0 %collective-permute-start.65 = (f32[8,128]{1,0:T(8,128)S(1)}, f32[8,128]{1,0:T(8,128)S(1)}, u32[]{:S(2)}, u32[]{:S(2)}) collective-permute-start(f32[8,128]{1,0:T(8,128)S(1)} %get-tuple-element.4), channel_id=1, source_target_pairs={{0,128},{32,160},{64,192},{96,224},{128,256},{160,288},{192,320},{... | collective-permute-start | bytes 12296 | tf_op jit(solution)/shard_map/ppermute | solution.py:27
  327.7 2.2 collective-permute-start.66
  332.5 14.4 %collective-permute-start.69 = (f32[8,128]{1,0:T(8,128)S(1)}, f32[8,128]{1,0:T(8,128)S(1)}, u32[]{:S(2)}, u32[]{:S(2)}) collective-permute-start(f32[8,128]{1,0:T(8,128)S(1)} %get-tuple-element.2), channel_id=1, source_target_pairs={{0,256},{32,288},{64,320},{96,352},{128,384},{160,416},{192,448},{... | collective-permute-start | bytes 12296 | tf_op jit(solution)/shard_map/ppermute | solution.py:27
  348.3 13.3 %collective-permute-start.68 = (f32[8,128]{1,0:T(8,128)S(1)}, f32[8,128]{1,0:T(8,128)S(1)}, u32[]{:S(2)}, u32[]{:S(2)}) collective-permute-start(f32[8,128]{1,0:T(8,128)S(1)} %get-tuple-element.283), channel_id=1, source_target_pairs={{0,256},{32,288},{64,320},{96,352},{128,384},{160,416},{192,448},{... | collective-permute-start | bytes 12296 | tf_op jit(solution)/shard_map/ppermute | solution.py:27
  362.9 13.3 %collective-permute-start.73 = (f32[8,128]{1,0:T(8,128)S(1)}, f32[8,128]{1,0:T(8,128)S(1)}, u32[]{:S(2)}, u32[]{:S(2)}) collective-permute-start(f32[8,128]{1,0:T(8,128)S(1)} %get-tuple-element.282), channel_id=1, source_target_pairs={{0,256},{32,288},{64,320},{96,352},{128,384},{160,416},{192,448},{... | collective-permute-start | bytes 12296 | tf_op jit(solution)/shard_map/ppermute | solution.py:27
  377.5 12.9 %collective-permute-done.74 = f32[8,128]{1,0:T(8,128)S(1)} collective-permute-done((f32[8,128]{1,0:T(8,128)S(1)}, f32[8,128]{1,0:T(8,128)S(1)}, u32[]{:S(2)}, u32[]{:S(2)}) %collective-permute-start.74) | collective-permute-done | bytes 4128 | tf_op jit(solution)/shard_map/ppermute | solution.py:27
  394.5 4.4 %collective-permute-done.76 = f32[1,8,128]{2,1,0:T(8,128)S(1)} collective-permute-done((f32[1,8,128]{2,1,0:T(8,128)S(1)}, f32[1,8,128]{2,1,0:T(8,128)S(1)}, u32[]{:S(2)}, u32[]{:S(2)}) %collective-permute-start.76) | collective-permute-done | bytes 4128 | tf_op jit(solution)/shard_map/ppermute | solution.py:27
  (242 shorter events, 72.4 us)
Async XLA Ops:
  2.4 18.0 %collective-permute-start.2 = (f32[1,2,8,128]{3,2,0,1:T(8,128)S(1)}, f32[1,2,8,128]{3,2,0,1:T(8,128)S(1)}, u32[]{:S(2)}, u32[]{:S(2)}) collective-permute-start(f32[1,2,8,128]{3,2,0,1:T(8,128)S(1)} %get-tuple-element.160), channel_id=1, source_target_pairs={{32,0},{64,32},{96,64},{128,96},{160,128},{192,160},{224,192},{256... | collective-permute-start | bytes 24584 | tf_op jit(solution)/shard_map/ppermute | solution.py:19
  3.8 16.6 %collective-permute-start.3 = (f32[1,2,8,128]{3,2,0,1:T(8,128)S(1)}, f32[1,2,8,128]{3,2,0,1:T(8,128)S(1)}, u32[]{:S(2)}, u32[]{:S(2)}) collective-permute-start(f32[1,2,8,128]{3,2,0,1:T(8,128)S(1)} %get-tuple-element.161), channel_id=1, source_target_pairs={{0,32},{32,64},{64,96},{96,128},{128,160},{160,192},{192,224},{224... | collective-permute-start | bytes 24584 | tf_op jit(solution)/shard_map/ppermute | solution.py:18
  32.9 14.6 %collective-permute-start.10 = (f32[8,128]{1,0:T(8,128)S(1)}, f32[8,128]{1,0:T(8,128)S(1)}, u32[]{:S(2)}, u32[]{:S(2)}) collective-permute-start(f32[8,128]{1,0:T(8,128)S(1)} %get-tuple-element.55), channel_id=1, source_target_pairs={{32,0},{64,32},{96,64},{128,96},{160,128},{192,160},{224,192},{256... | collective-permute-start | bytes 12296 | tf_op jit(solution)/shard_map/ppermute | solution.py:27
  34.2 13.3 %collective-permute-start.7 = (f32[8,128]{1,0:T(8,128)S(1)}, f32[8,128]{1,0:T(8,128)S(1)}, u32[]{:S(2)}, u32[]{:S(2)}) collective-permute-start(f32[8,128]{1,0:T(8,128)S(1)} %get-tuple-element.55), channel_id=1, source_target_pairs={{0,32},{32,64},{64,96},{96,128},{128,160},{160,192},{192,224},{224... | collective-permute-start | bytes 12296 | tf_op jit(solution)/shard_map/ppermute | solution.py:27
  48.8 22.2 %collective-permute-start.13 = (f32[8,128]{1,0:T(8,128)S(1)}, f32[8,128]{1,0:T(8,128)S(1)}, u32[]{:S(2)}, u32[]{:S(2)}) collective-permute-start(f32[8,128]{1,0:T(8,128)S(1)} %get-tuple-element.51), channel_id=1, source_target_pairs={{0,32},{32,64},{64,96},{96,128},{128,160},{160,192},{192,224},{224... | collective-permute-start | bytes 12296 | tf_op jit(solution)/shard_map/ppermute | solution.py:27
  53.9 18.4 %collective-permute-start.14 = (f32[8,128]{1,0:T(8,128)S(1)}, f32[8,128]{1,0:T(8,128)S(1)}, u32[]{:S(2)}, u32[]{:S(2)}) collective-permute-start(f32[8,128]{1,0:T(8,128)S(1)} %get-tuple-element.52), channel_id=1, source_target_pairs={{32,0},{64,32},{96,64},{128,96},{160,128},{192,160},{224,192},{256... | collective-permute-start | bytes 12296 | tf_op jit(solution)/shard_map/ppermute | solution.py:27
  55.2 25.5 %collective-permute-start.12 = (f32[8,128]{1,0:T(8,128)S(1)}, f32[8,128]{1,0:T(8,128)S(1)}, u32[]{:S(2)}, u32[]{:S(2)}) collective-permute-start(f32[8,128]{1,0:T(8,128)S(1)} %get-tuple-element.52), channel_id=1, source_target_pairs={{0,32},{32,64},{64,96},{96,128},{128,160},{160,192},{192,224},{224... | collective-permute-start | bytes 12296 | tf_op jit(solution)/shard_map/ppermute | solution.py:27
  61.0 21.1 %collective-permute-start.17 = (f32[8,128]{1,0:T(8,128)S(1)}, f32[8,128]{1,0:T(8,128)S(1)}, u32[]{:S(2)}, u32[]{:S(2)}) collective-permute-start(f32[8,128]{1,0:T(8,128)S(1)} %get-tuple-element.51), channel_id=1, source_target_pairs={{32,0},{64,32},{96,64},{128,96},{160,128},{192,160},{224,192},{256... | collective-permute-start | bytes 12296 | tf_op jit(solution)/shard_map/ppermute | solution.py:27
  62.3 19.8 %collective-permute-start.16 = (f32[8,128]{1,0:T(8,128)S(1)}, f32[8,128]{1,0:T(8,128)S(1)}, u32[]{:S(2)}, u32[]{:S(2)}) collective-permute-start(f32[8,128]{1,0:T(8,128)S(1)} %get-tuple-element.50), channel_id=1, source_target_pairs={{0,64},{32,96},{64,128},{96,160},{128,192},{160,224},{192,256},{22... | collective-permute-start | bytes 12296 | tf_op jit(solution)/shard_map/ppermute | solution.py:27
  71.0 11.1 %collective-permute-start.19 = (f32[8,128]{1,0:T(8,128)S(1)}, f32[8,128]{1,0:T(8,128)S(1)}, u32[]{:S(2)}, u32[]{:S(2)}) collective-permute-start(f32[8,128]{1,0:T(8,128)S(1)} %get-tuple-element.50), channel_id=1, source_target_pairs={{64,0},{96,32},{128,64},{160,96},{192,128},{224,160},{256,192},{28... | collective-permute-start | bytes 12296 | tf_op jit(solution)/shard_map/ppermute | solution.py:27
  88.4 25.2 %collective-permute-start.21 = (f32[8,128]{1,0:T(8,128)S(1)}, f32[8,128]{1,0:T(8,128)S(1)}, u32[]{:S(2)}, u32[]{:S(2)}) collective-permute-start(f32[8,128]{1,0:T(8,128)S(1)} %get-tuple-element.48), channel_id=1, source_target_pairs={{0,64},{32,96},{64,128},{96,160},{128,192},{160,224},{192,256},{22... | collective-permute-start | bytes 12296 | tf_op jit(solution)/shard_map/ppermute | solution.py:27
  94.6 20.3 %collective-permute-start.22 = (f32[8,128]{1,0:T(8,128)S(1)}, f32[8,128]{1,0:T(8,128)S(1)}, u32[]{:S(2)}, u32[]{:S(2)}) collective-permute-start(f32[8,128]{1,0:T(8,128)S(1)} %get-tuple-element.49), channel_id=1, source_target_pairs={{64,0},{96,32},{128,64},{160,96},{192,128},{224,160},{256,192},{28... | collective-permute-start | bytes 12296 | tf_op jit(solution)/shard_map/ppermute | solution.py:27
  95.9 27.5 %collective-permute-start.20 = (f32[8,128]{1,0:T(8,128)S(1)}, f32[8,128]{1,0:T(8,128)S(1)}, u32[]{:S(2)}, u32[]{:S(2)}) collective-permute-start(f32[8,128]{1,0:T(8,128)S(1)} %get-tuple-element.49), channel_id=1, source_target_pairs={{0,64},{32,96},{64,128},{96,160},{128,192},{160,224},{192,256},{22... | collective-permute-start | bytes 12296 | tf_op jit(solution)/shard_map/ppermute | solution.py:27
  102.1 22.7 %collective-permute-start.25 = (f32[8,128]{1,0:T(8,128)S(1)}, f32[8,128]{1,0:T(8,128)S(1)}, u32[]{:S(2)}, u32[]{:S(2)}) collective-permute-start(f32[8,128]{1,0:T(8,128)S(1)} %get-tuple-element.48), channel_id=1, source_target_pairs={{64,0},{96,32},{128,64},{160,96},{192,128},{224,160},{256,192},{28... | collective-permute-start | bytes 12296 | tf_op jit(solution)/shard_map/ppermute | solution.py:27
  103.4 21.3 %collective-permute-start.24 = (f32[8,128]{1,0:T(8,128)S(1)}, f32[8,128]{1,0:T(8,128)S(1)}, u32[]{:S(2)}, u32[]{:S(2)}) collective-permute-start(f32[8,128]{1,0:T(8,128)S(1)} %get-tuple-element.47), channel_id=1, source_target_pairs={{0,128},{32,160},{64,192},{96,224},{128,256},{160,288},{192,320},{... | collective-permute-start | bytes 12296 | tf_op jit(solution)/shard_map/ppermute | solution.py:27
  113.6 11.1 %collective-permute-start.27 = (f32[8,128]{1,0:T(8,128)S(1)}, f32[8,128]{1,0:T(8,128)S(1)}, u32[]{:S(2)}, u32[]{:S(2)}) collective-permute-start(f32[8,128]{1,0:T(8,128)S(1)} %get-tuple-element.47), channel_id=1, source_target_pairs={{128,0},{160,32},{192,64},{224,96},{256,128},{288,160},{320,192},{... | collective-permute-start | bytes 12296 | tf_op jit(solution)/shard_map/ppermute | solution.py:27
  132.8 29.7 %collective-permute-start.28 = (f32[8,128]{1,0:T(8,128)S(1)}, f32[8,128]{1,0:T(8,128)S(1)}, u32[]{:S(2)}, u32[]{:S(2)}) collective-permute-start(f32[8,128]{1,0:T(8,128)S(1)} %get-tuple-element.46), channel_id=1, source_target_pairs={{0,128},{32,160},{64,192},{96,224},{128,256},{160,288},{192,320},{... | collective-permute-start | bytes 12296 | tf_op jit(solution)/shard_map/ppermute | solution.py:27
  140.0 23.8 %collective-permute-start.29 = (f32[8,128]{1,0:T(8,128)S(1)}, f32[8,128]{1,0:T(8,128)S(1)}, u32[]{:S(2)}, u32[]{:S(2)}) collective-permute-start(f32[8,128]{1,0:T(8,128)S(1)} %get-tuple-element.45), channel_id=1, source_target_pairs={{0,128},{32,160},{64,192},{96,224},{128,256},{160,288},{192,320},{... | collective-permute-start | bytes 12296 | tf_op jit(solution)/shard_map/ppermute | solution.py:27
  145.5 18.4 %collective-permute-start.30 = (f32[8,128]{1,0:T(8,128)S(1)}, f32[8,128]{1,0:T(8,128)S(1)}, u32[]{:S(2)}, u32[]{:S(2)}) collective-permute-start(f32[8,128]{1,0:T(8,128)S(1)} %get-tuple-element.46), channel_id=1, source_target_pairs={{128,0},{160,32},{192,64},{224,96},{256,128},{288,160},{320,192},{... | collective-permute-start | bytes 12296 | tf_op jit(solution)/shard_map/ppermute | solution.py:27
  146.8 17.1 %collective-permute-start.33 = (f32[8,128]{1,0:T(8,128)S(1)}, f32[8,128]{1,0:T(8,128)S(1)}, u32[]{:S(2)}, u32[]{:S(2)}) collective-permute-start(f32[8,128]{1,0:T(8,128)S(1)} %get-tuple-element.45), channel_id=1, source_target_pairs={{128,0},{160,32},{192,64},{224,96},{256,128},{288,160},{320,192},{... | collective-permute-start | bytes 12296 | tf_op jit(solution)/shard_map/ppermute | solution.py:27
  148.1 43.6 %collective-permute-start.32 = (f32[8,128]{1,0:T(8,128)S(1)}, f32[8,128]{1,0:T(8,128)S(1)}, u32[]{:S(2)}, u32[]{:S(2)}) collective-permute-start(f32[8,128]{1,0:T(8,128)S(1)} %get-tuple-element.44), channel_id=1, source_target_pairs={{0,256},{32,288},{64,320},{96,352},{128,384},{160,416},{192,448},{... | collective-permute-start | bytes 12296 | tf_op jit(solution)/shard_map/ppermute | solution.py:27
  162.5 30.5 %collective-permute-start.35 = (f32[8,128]{1,0:T(8,128)S(1)}, f32[8,128]{1,0:T(8,128)S(1)}, u32[]{:S(2)}, u32[]{:S(2)}) collective-permute-start(f32[8,128]{1,0:T(8,128)S(1)} %get-tuple-element.44), channel_id=1, source_target_pairs={{256,0},{288,32},{320,64},{352,96},{384,128},{416,160},{448,192},{... | collective-permute-start | bytes 12296 | tf_op jit(solution)/shard_map/ppermute | solution.py:27
  163.9 29.2 %collective-permute-start.31 = (f32[8,128]{1,0:T(8,128)S(1)}, f32[8,128]{1,0:T(8,128)S(1)}, u32[]{:S(2)}, u32[]{:S(2)}) collective-permute-start(f32[8,128]{1,0:T(8,128)S(1)} %get-tuple-element.286), channel_id=1, source_target_pairs={{0,256},{32,288},{64,320},{96,352},{128,384},{160,416},{192,448},{... | collective-permute-start | bytes 12296 | tf_op jit(solution)/shard_map/ppermute | solution.py:27
  177.2 15.9 %collective-permute-start.34 = (f32[8,128]{1,0:T(8,128)S(1)}, f32[8,128]{1,0:T(8,128)S(1)}, u32[]{:S(2)}, u32[]{:S(2)}) collective-permute-start(f32[8,128]{1,0:T(8,128)S(1)} %get-tuple-element.286), channel_id=1, source_target_pairs={{256,0},{288,32},{320,64},{352,96},{384,128},{416,160},{448,192},{... | collective-permute-start | bytes 12296 | tf_op jit(solution)/shard_map/ppermute | solution.py:27
  178.5 14.6 %collective-permute-start.36 = (f32[8,128]{1,0:T(8,128)S(1)}, f32[8,128]{1,0:T(8,128)S(1)}, u32[]{:S(2)}, u32[]{:S(2)}) collective-permute-start(f32[8,128]{1,0:T(8,128)S(1)} %get-tuple-element.285), channel_id=1, source_target_pairs={{0,256},{32,288},{64,320},{96,352},{128,384},{160,416},{192,448},{... | collective-permute-start | bytes 12296 | tf_op jit(solution)/shard_map/ppermute | solution.py:27
  191.7 14.2 %collective-permute-start.37 = (f32[8,128]{1,0:T(8,128)S(1)}, f32[8,128]{1,0:T(8,128)S(1)}, u32[]{:S(2)}, u32[]{:S(2)}) collective-permute-start(f32[8,128]{1,0:T(8,128)S(1)} %get-tuple-element.287), channel_id=1, source_target_pairs={{256,0},{288,32},{320,64},{352,96},{384,128},{416,160},{448,192},{... | collective-permute-start | bytes 12296 | tf_op jit(solution)/shard_map/ppermute | solution.py:27
  227.9 13.0 %collective-permute-start.44 = (f32[8,128]{1,0:T(8,128)S(1)}, f32[8,128]{1,0:T(8,128)S(1)}, u32[]{:S(2)}, u32[]{:S(2)}) collective-permute-start(f32[8,128]{1,0:T(8,128)S(1)} %get-tuple-element.13), channel_id=1, source_target_pairs={{0,32},{32,64},{64,96},{96,128},{128,160},{160,192},{192,224},{224... | collective-permute-start | bytes 12296 | tf_op jit(solution)/shard_map/ppermute | solution.py:27
  246.3 19.5 %collective-permute-start.50 = (f32[8,128]{1,0:T(8,128)S(1)}, f32[8,128]{1,0:T(8,128)S(1)}, u32[]{:S(2)}, u32[]{:S(2)}) collective-permute-start(f32[8,128]{1,0:T(8,128)S(1)} %get-tuple-element.9), channel_id=1, source_target_pairs={{0,32},{32,64},{64,96},{96,128},{128,160},{160,192},{192,224},{224... | collective-permute-start | bytes 12296 | tf_op jit(solution)/shard_map/ppermute | solution.py:27
  250.3 16.9 %collective-permute-start.51 = (f32[8,128]{1,0:T(8,128)S(1)}, f32[8,128]{1,0:T(8,128)S(1)}, u32[]{:S(2)}, u32[]{:S(2)}) collective-permute-start(f32[8,128]{1,0:T(8,128)S(1)} %get-tuple-element.10), channel_id=1, source_target_pairs={{32,0},{64,32},{96,64},{128,96},{160,128},{192,160},{224,192},{256... | collective-permute-start | bytes 12296 | tf_op jit(solution)/shard_map/ppermute | solution.py:27
  251.6 22.8 %collective-permute-start.49 = (f32[8,128]{1,0:T(8,128)S(1)}, f32[8,128]{1,0:T(8,128)S(1)}, u32[]{:S(2)}, u32[]{:S(2)}) collective-permute-start(f32[8,128]{1,0:T(8,128)S(1)} %get-tuple-element.10), channel_id=1, source_target_pairs={{0,32},{32,64},{64,96},{96,128},{128,160},{160,192},{192,224},{224... | collective-permute-start | bytes 12296 | tf_op jit(solution)/shard_map/ppermute | solution.py:27
  257.3 18.4 %collective-permute-start.54 = (f32[8,128]{1,0:T(8,128)S(1)}, f32[8,128]{1,0:T(8,128)S(1)}, u32[]{:S(2)}, u32[]{:S(2)}) collective-permute-start(f32[8,128]{1,0:T(8,128)S(1)} %get-tuple-element.9), channel_id=1, source_target_pairs={{32,0},{64,32},{96,64},{128,96},{160,128},{192,160},{224,192},{256... | collective-permute-start | bytes 12296 | tf_op jit(solution)/shard_map/ppermute | solution.py:27
  258.6 17.1 %collective-permute-start.53 = (f32[8,128]{1,0:T(8,128)S(1)}, f32[8,128]{1,0:T(8,128)S(1)}, u32[]{:S(2)}, u32[]{:S(2)}) collective-permute-start(f32[8,128]{1,0:T(8,128)S(1)} %get-tuple-element.8), channel_id=1, source_target_pairs={{0,64},{32,96},{64,128},{96,160},{128,192},{160,224},{192,256},{22... | collective-permute-start | bytes 12296 | tf_op jit(solution)/shard_map/ppermute | solution.py:27
  282.1 21.4 %collective-permute-start.58 = (f32[8,128]{1,0:T(8,128)S(1)}, f32[8,128]{1,0:T(8,128)S(1)}, u32[]{:S(2)}, u32[]{:S(2)}) collective-permute-start(f32[8,128]{1,0:T(8,128)S(1)} %get-tuple-element.6), channel_id=1, source_target_pairs={{0,64},{32,96},{64,128},{96,160},{128,192},{160,224},{192,256},{22... | collective-permute-start | bytes 12296 | tf_op jit(solution)/shard_map/ppermute | solution.py:27
  288.1 16.7 %collective-permute-start.59 = (f32[8,128]{1,0:T(8,128)S(1)}, f32[8,128]{1,0:T(8,128)S(1)}, u32[]{:S(2)}, u32[]{:S(2)}) collective-permute-start(f32[8,128]{1,0:T(8,128)S(1)} %get-tuple-element.7), channel_id=1, source_target_pairs={{64,0},{96,32},{128,64},{160,96},{192,128},{224,160},{256,192},{28... | collective-permute-start | bytes 12296 | tf_op jit(solution)/shard_map/ppermute | solution.py:27
  289.4 23.9 %collective-permute-start.57 = (f32[8,128]{1,0:T(8,128)S(1)}, f32[8,128]{1,0:T(8,128)S(1)}, u32[]{:S(2)}, u32[]{:S(2)}) collective-permute-start(f32[8,128]{1,0:T(8,128)S(1)} %get-tuple-element.7), channel_id=1, source_target_pairs={{0,64},{32,96},{64,128},{96,160},{128,192},{160,224},{192,256},{22... | collective-permute-start | bytes 12296 | tf_op jit(solution)/shard_map/ppermute | solution.py:27
  294.8 19.8 %collective-permute-start.62 = (f32[8,128]{1,0:T(8,128)S(1)}, f32[8,128]{1,0:T(8,128)S(1)}, u32[]{:S(2)}, u32[]{:S(2)}) collective-permute-start(f32[8,128]{1,0:T(8,128)S(1)} %get-tuple-element.6), channel_id=1, source_target_pairs={{64,0},{96,32},{128,64},{160,96},{192,128},{224,160},{256,192},{28... | collective-permute-start | bytes 12296 | tf_op jit(solution)/shard_map/ppermute | solution.py:27
  296.1 18.4 %collective-permute-start.61 = (f32[8,128]{1,0:T(8,128)S(1)}, f32[8,128]{1,0:T(8,128)S(1)}, u32[]{:S(2)}, u32[]{:S(2)}) collective-permute-start(f32[8,128]{1,0:T(8,128)S(1)} %get-tuple-element.5), channel_id=1, source_target_pairs={{0,128},{32,160},{64,192},{96,224},{128,256},{160,288},{192,320},{... | collective-permute-start | bytes 12296 | tf_op jit(solution)/shard_map/ppermute | solution.py:27
  303.5 11.1 %collective-permute-start.64 = (f32[8,128]{1,0:T(8,128)S(1)}, f32[8,128]{1,0:T(8,128)S(1)}, u32[]{:S(2)}, u32[]{:S(2)}) collective-permute-start(f32[8,128]{1,0:T(8,128)S(1)} %get-tuple-element.5), channel_id=1, source_target_pairs={{128,0},{160,32},{192,64},{224,96},{256,128},{288,160},{320,192},{... | collective-permute-start | bytes 12296 | tf_op jit(solution)/shard_map/ppermute | solution.py:27
  322.7 24.2 %collective-permute-start.65 = (f32[8,128]{1,0:T(8,128)S(1)}, f32[8,128]{1,0:T(8,128)S(1)}, u32[]{:S(2)}, u32[]{:S(2)}) collective-permute-start(f32[8,128]{1,0:T(8,128)S(1)} %get-tuple-element.4), channel_id=1, source_target_pairs={{0,128},{32,160},{64,192},{96,224},{128,256},{160,288},{192,320},{... | collective-permute-start | bytes 12296 | tf_op jit(solution)/shard_map/ppermute | solution.py:27
  327.7 20.6 %collective-permute-start.66 = (f32[8,128]{1,0:T(8,128)S(1)}, f32[8,128]{1,0:T(8,128)S(1)}, u32[]{:S(2)}, u32[]{:S(2)}) collective-permute-start(f32[8,128]{1,0:T(8,128)S(1)} %get-tuple-element.3), channel_id=1, source_target_pairs={{0,128},{32,160},{64,192},{96,224},{128,256},{160,288},{192,320},{... | collective-permute-start | bytes 12296 | tf_op jit(solution)/shard_map/ppermute | solution.py:27
  329.9 18.4 %collective-permute-start.67 = (f32[8,128]{1,0:T(8,128)S(1)}, f32[8,128]{1,0:T(8,128)S(1)}, u32[]{:S(2)}, u32[]{:S(2)}) collective-permute-start(f32[8,128]{1,0:T(8,128)S(1)} %get-tuple-element.4), channel_id=1, source_target_pairs={{128,0},{160,32},{192,64},{224,96},{256,128},{288,160},{320,192},{... | collective-permute-start | bytes 12296 | tf_op jit(solution)/shard_map/ppermute | solution.py:27
  331.2 17.1 %collective-permute-start.70 = (f32[8,128]{1,0:T(8,128)S(1)}, f32[8,128]{1,0:T(8,128)S(1)}, u32[]{:S(2)}, u32[]{:S(2)}) collective-permute-start(f32[8,128]{1,0:T(8,128)S(1)} %get-tuple-element.3), channel_id=1, source_target_pairs={{128,0},{160,32},{192,64},{224,96},{256,128},{288,160},{320,192},{... | collective-permute-start | bytes 12296 | tf_op jit(solution)/shard_map/ppermute | solution.py:27
  332.5 43.6 %collective-permute-start.69 = (f32[8,128]{1,0:T(8,128)S(1)}, f32[8,128]{1,0:T(8,128)S(1)}, u32[]{:S(2)}, u32[]{:S(2)}) collective-permute-start(f32[8,128]{1,0:T(8,128)S(1)} %get-tuple-element.2), channel_id=1, source_target_pairs={{0,256},{32,288},{64,320},{96,352},{128,384},{160,416},{192,448},{... | collective-permute-start | bytes 12296 | tf_op jit(solution)/shard_map/ppermute | solution.py:27
  347.0 30.5 %collective-permute-start.72 = (f32[8,128]{1,0:T(8,128)S(1)}, f32[8,128]{1,0:T(8,128)S(1)}, u32[]{:S(2)}, u32[]{:S(2)}) collective-permute-start(f32[8,128]{1,0:T(8,128)S(1)} %get-tuple-element.2), channel_id=1, source_target_pairs={{256,0},{288,32},{320,64},{352,96},{384,128},{416,160},{448,192},{... | collective-permute-start | bytes 12296 | tf_op jit(solution)/shard_map/ppermute | solution.py:27
  348.3 29.2 %collective-permute-start.68 = (f32[8,128]{1,0:T(8,128)S(1)}, f32[8,128]{1,0:T(8,128)S(1)}, u32[]{:S(2)}, u32[]{:S(2)}) collective-permute-start(f32[8,128]{1,0:T(8,128)S(1)} %get-tuple-element.283), channel_id=1, source_target_pairs={{0,256},{32,288},{64,320},{96,352},{128,384},{160,416},{192,448},{... | collective-permute-start | bytes 12296 | tf_op jit(solution)/shard_map/ppermute | solution.py:27
  361.6 15.9 %collective-permute-start.71 = (f32[8,128]{1,0:T(8,128)S(1)}, f32[8,128]{1,0:T(8,128)S(1)}, u32[]{:S(2)}, u32[]{:S(2)}) collective-permute-start(f32[8,128]{1,0:T(8,128)S(1)} %get-tuple-element.283), channel_id=1, source_target_pairs={{256,0},{288,32},{320,64},{352,96},{384,128},{416,160},{448,192},{... | collective-permute-start | bytes 12296 | tf_op jit(solution)/shard_map/ppermute | solution.py:27
  362.9 14.6 %collective-permute-start.73 = (f32[8,128]{1,0:T(8,128)S(1)}, f32[8,128]{1,0:T(8,128)S(1)}, u32[]{:S(2)}, u32[]{:S(2)}) collective-permute-start(f32[8,128]{1,0:T(8,128)S(1)} %get-tuple-element.282), channel_id=1, source_target_pairs={{0,256},{32,288},{64,320},{96,352},{128,384},{160,416},{192,448},{... | collective-permute-start | bytes 12296 | tf_op jit(solution)/shard_map/ppermute | solution.py:27
  376.2 14.2 %collective-permute-start.74 = (f32[8,128]{1,0:T(8,128)S(1)}, f32[8,128]{1,0:T(8,128)S(1)}, u32[]{:S(2)}, u32[]{:S(2)}) collective-permute-start(f32[8,128]{1,0:T(8,128)S(1)} %get-tuple-element.284), channel_id=1, source_target_pairs={{256,0},{288,32},{320,64},{352,96},{384,128},{416,160},{448,192},{... | collective-permute-start | bytes 12296 | tf_op jit(solution)/shard_map/ppermute | solution.py:27
  (34 other events, 349.5 us)
where the time goes:
time: 402 us; the launch traced here: 400 us
  starting transfers between devices  305 us (76%)
  waiting for transfers between devices  84.5 us (21%)
  other arithmetic  5.41 us (1%)
    ppermute x71, starting transfers between devices, from_behind(): return lax.ppermute(block, axis, route)  285 us
    ppermute x71, waiting for transfers between devices, from_behind(): return lax.ppermute(block, axis, route)  79.4 us
    ppermute x3, starting transfers between devices, padded(): before = lax.ppermute(last, axis, up)  11.3 us
    ppermute x3, starting transfers between devices, padded(): after = lax.ppermute(initial, axis, down)  8.47 us
  transfers between devices with their start and end apart: 77, of which 20 were waited for; matrix products, arithmetic and copies ran while one was open for 0% of the time, Pallas kernels for 0%

commit v1 on v0

v1 whole, which is shorter than its diff:
```python
import functools

import jax
import jax.numpy as jnp
from jax import lax
from jax.experimental import pallas as pl
from jax.experimental.pallas import tpu as pltpu
from jax.sharding import PartitionSpec as P

MESH = pl.DeviceIdType.MESH
CELLS = 32
COEFS = 6
FIRST_ROOT = 5
SECOND_ROOT = 0


def resistivity(field, base_cond):
    square = field * field
    return (1.0 + square) / (base_cond * (1.0 + 2.0 * square))


def kernel(
    parts,
    rows,
    h_ref,
    f_ref,
    k_ref,
    s_ref,
    u_out,
    flux_out,
    q_ref,
    r_ref,
    rho_ref,
    edge,
    edge_in,
    head,
    head_in,
    coef,
    gather,
    state_out,
    state,
    y_send,
    y_recv,
    x_send,
    x_recv,
    c_send,
    c_recv,
    s_send,
    s_recv,
):
    gx = lax.axis_index("gx")
    gy = lax.axis_index("gy")
    first_root = FIRST_ROOT % parts
    second_root = SECOND_ROOT % parts
    roots = (first_root, second_root)
    next_y = lax.rem(gy + 1, rows)
    prev_y = lax.rem(gy + rows - 1, rows)
    has_up = gx < parts - 1
    has_down = gx > 0

    barrier = pltpu.get_barrier_semaphore()

    def greet(target):
        pl.semaphore_signal(barrier, inc=1, device_id=target, device_id_type=MESH)

    greet({"gy": next_y})
    greet({"gy": prev_y})

    @pl.when(has_up)
    def _():
        greet({"gx": gx + 1})

    @pl.when(has_down)
    def _():
        greet({"gx": gx - 1})

    for root in roots:

        @pl.when(gx == root)
        def _():
            for step in range(1, parts):
                greet({"gx": lax.rem(gx + step, parts)})

    greetings = 2 + has_up.astype(jnp.int32) + has_down.astype(jnp.int32)
    for root in roots:
        greetings = greetings + (gx != root).astype(jnp.int32)

    lane = lax.broadcasted_iota(jnp.int32, (8, 128), 1)
    plane = lax.broadcasted_iota(jnp.int32, (8, 128), 0)
    even = lane % 2 == 0
    pair = lane // 2

    packed = jnp.zeros((8, 128), jnp.float32)
    for i in range(CELLS):
        field = f_ref[i]
        q = resistivity(field, k_ref[i])
        q_ref[i] = q
        packed = jnp.where(pair == i, pltpu.roll(field, 2 * i + 1, 1), packed)
        packed = jnp.where(pair == i + 32, pltpu.roll(q, (64 + 2 * i + 1) % 128, 1), packed)
    edge[...] = packed
    head[0] = f_ref[0]
    head[1] = k_ref[0]
    head[2] = jnp.full((8, 128), h_ref[0], jnp.float32)

    pl.semaphore_wait(barrier, greetings)

    def y_copy(slot, target):
        return pltpu.make_async_remote_copy(
            src_ref=edge,
            dst_ref=edge_in.at[slot],
            send_sem=y_send.at[slot],
            recv_sem=y_recv.at[slot],
            device_id={"gy": target},
            device_id_type=MESH,
        )

    to_next = y_copy(0, next_y)
    to_prev = y_copy(1, prev_y)
    to_next.start()
    to_prev.start()
    to_down = pltpu.make_async_remote_copy(
        src_ref=head,
        dst_ref=head_in,
        send_sem=x_send,
        recv_sem=x_recv,
        device_id={"gx": lax.rem(gx + parts - 1, parts)},
        device_id_type=MESH,
    )

    @pl.when(has_down)
    def _():
        to_down.start()

    for i in range(CELLS):
        field, q = f_ref[i], q_ref[i]
        face_y = 0.3 / (q + pltpu.roll(q, 127, 1)) * (pltpu.roll(field, 127, 1) - field)
        face_y = jnp.where(lane == 127, 0.0, face_y)
        face_z = 0.2 / (q + pltpu.roll(q, 7, 0)) * (pltpu.roll(field, 7, 0) - field)
        face_z = jnp.where(plane == 7, 0.0, face_z)
        r_ref[i] = (
            field
            + (face_y - pltpu.roll(face_y, 1, 1))
            + (face_z - pltpu.roll(face_z, 1, 0))
            + s_ref[i]
        )

    h = [h_ref[i] for i in range(CELLS)]
    is_first = gx == 0
    is_last = gx == parts - 1

    def face_weights(q_next, h_next):
        scale = 1.0 / (16.0 * CELLS * CELLS)
        for i in range(CELLS - 1):
            rho_ref[i] = ((h[i] + h[i + 1]) * scale) * (q_ref[i] + q_ref[i + 1])
        q_last = q_ref[CELLS - 1]
        q_next = jnp.where(is_last, q_last, q_next)
        h_next = jnp.where(is_last, h[CELLS - 1], h_next)
        rho_ref[CELLS - 1] = ((h[CELLS - 1] + h_next) * scale) * (q_last + q_next)
        return jnp.where(is_first, (4.0 * h[0] * scale) * q_ref[0], 0.0)

    def transfer(rho_start, slot):
        one = jnp.ones((8, 128), jnp.float32)
        zero = jnp.zeros((8, 128), jnp.float32)
        u_a, f_a = one, zero
        u_b, f_b = zero - rho_start, one
        u_c, f_c = zero, zero
        for i in range(CELLS):
            rho = rho_ref[i]
            f_a = f_a - h[i] * u_a
            f_b = f_b - h[i] * u_b
            f_c = f_c + (r_ref[i] - h[i] * u_c)
            u_a = u_a - rho * f_a
            u_b = u_b - rho * f_b
            u_c = u_c - rho * f_c
        for c, value in enumerate((u_a, u_b, f_a, f_b, u_c, f_c)):
            coef[slot, c] = value

    def solve(root, slot):
        here = gx == root
        to_root = pltpu.make_async_remote_copy(
            src_ref=coef.at[slot],
            dst_ref=gather.at[slot, gx],
            send_sem=c_send.at[slot],
            recv_sem=c_recv.at[slot],
            device_id={"gx": root},
            device_id_type=MESH,
        )

        @pl.when(jnp.logical_not(here))
        def _():
            to_root.start()

        @pl.when(here)
        def _():
            gather[slot, root] = coef[slot]
            arrived = gather.at[slot, pl.ds(0, parts - 1)]
            pltpu.make_async_copy(arrived, arrived, c_recv.at[slot]).wait()
            zero = jnp.zeros((8, 128), jnp.float32)
            w_u, w_f = zero, zero + 1.0
            p_u, p_f = zero, zero
            entries = []
            for part in range(parts):
                entries.append((w_u, w_f, p_u, p_f))
                m11, m12, m21, m22, b_u, b_f = (gather[slot, part, c] for c in range(COEFS))
                w_u, w_f = m11 * w_u + m12 * w_f, m21 * w_u + m22 * w_f
                p_u, p_f = m11 * p_u + m12 * p_f + b_u, m21 * p_u + m22 * p_f + b_f
            start = -p_u / w_u
            for part, (w_u, w_f, p_u, p_f) in enumerate(entries):
                state_out[slot, part, 0] = w_u * start + p_u
                state_out[slot, part, 1] = w_f * start + p_f
            order = sorted(
                (part for part in range(parts) if part != root),
                key=lambda part: -min((part - root) % parts, (root - part) % parts),
            )
            for part in order:
                pltpu.make_async_remote_copy(
                    src_ref=state_out.at[slot, part],
                    dst_ref=state.at[slot],
                    send_sem=s_send.at[slot],
                    recv_sem=s_recv.at[slot],
                    device_id={"gx": part},
                    device_id_type=MESH,
                ).start()
            state[slot] = state_out[slot, root]

        @pl.when(jnp.logical_not(here))
        def _():
            pltpu.make_async_copy(state.at[slot], state.at[slot], s_recv.at[slot]).wait()

    def finish(root, slot):
        here = gx == root

        @pl.when(here)
        def _():
            sent = state_out.at[slot, pl.ds(0, parts - 1)]
            pltpu.make_async_copy(sent, sent, s_send.at[slot]).wait()

        @pl.when(jnp.logical_not(here))
        def _():
            pltpu.make_async_copy(coef.at[slot], coef.at[slot], c_send.at[slot]).wait()

    to_next.wait_recv()
    to_prev.wait_recv()
    own = pltpu.roll(packed, 127, 1)
    other = jnp.where(even, edge_in[0], pltpu.roll(edge_in[1], 126, 1))
    own_q = pltpu.roll(own, 64, 1)
    other_q = pltpu.roll(other, 64, 1)
    outside = jnp.logical_or(
        jnp.logical_and(even, gy == 0),
        jnp.logical_and(jnp.logical_not(even), gy == rows - 1),
    )
    face = jnp.where(outside, 0.0, 0.3 / (own_q + other_q) * (other - own))
    rim = jnp.logical_or(lane == 0, lane == 127)
    for i in range(CELLS):
        extra = jnp.where(rim, pltpu.roll(face, (128 - 2 * i) % 128, 1), 0.0)
        r_ref[i] = h[i] * (r_ref[i] + extra)

    @pl.when(has_up)
    def _():
        to_down.wait_recv()

    @pl.when(is_last)
    def _():
        head_in[...] = jnp.ones_like(head_in)

    h_next = head_in[2]
    rho_start = face_weights(resistivity(head_in[0], head_in[1]), h_next)
    transfer(rho_start, 0)
    solve(first_root, 0)

    u, flux = state[0, 0], state[0, 1]
    u = u - rho_start * flux
    for i in range(CELLS):
        flux = flux + (r_ref[i] - h[i] * u)
        q_ref[i] = resistivity(0.5 * (f_ref[i] + u), k_ref[i])
        u = u - rho_ref[i] * flux
    rho_start = face_weights(resistivity(0.5 * (head_in[0] + u), head_in[1]), h_next)
    transfer(rho_start, 1)
    solve(second_root, 1)

    u, flux = state[1, 0], state[1, 1]
    u = u - rho_start * flux
    for i in range(CELLS):
        flux = flux + (r_ref[i] - h[i] * u)
        u_out[i] = u
        flux_out[i] = flux * (1.0 / CELLS)
        u = u - rho_ref[i] * flux

    to_next.wait_send()
    to_prev.wait_send()

    @pl.when(has_down)
    def _():
        to_down.wait_send()

    finish(first_root, 0)
    finish(second_root, 1)


def per_device(parts, rows, field_now, base_cond, spacing, source):
    whole = pl.BlockSpec(memory_space=pltpu.VMEM)
    tile = (8, 128)
    shape = jax.ShapeDtypeStruct(field_now.shape, jnp.float32)
    return pl.pallas_call(
        functools.partial(kernel, parts, rows),
        out_shape=[shape, shape],
        in_specs=[pl.BlockSpec(memory_space=pltpu.SMEM), whole, whole, whole],
        out_specs=[whole, whole],
        scratch_shapes=[
            pltpu.VMEM((CELLS, *tile), jnp.float32),
            pltpu.VMEM((CELLS, *tile), jnp.float32),
            pltpu.VMEM((CELLS, *tile), jnp.float32),
            pltpu.VMEM(tile, jnp.float32),
            pltpu.VMEM((2, *tile), jnp.float32),
            pltpu.VMEM((3, *tile), jnp.float32),
            pltpu.VMEM((3, *tile), jnp.float32),
            pltpu.VMEM((2, COEFS, *tile), jnp.float32),
            pltpu.VMEM((2, parts, COEFS, *tile), jnp.float32),
            pltpu.VMEM((2, parts, 2, *tile), jnp.float32),
            pltpu.VMEM((2, 2, *tile), jnp.float32),
            pltpu.SemaphoreType.DMA((2,)),
            pltpu.SemaphoreType.DMA((2,)),
            pltpu.SemaphoreType.DMA,
            pltpu.SemaphoreType.DMA,
            pltpu.SemaphoreType.DMA((2,)),
            pltpu.SemaphoreType.DMA((2,)),
            pltpu.SemaphoreType.DMA((2,)),
            pltpu.SemaphoreType.DMA((2,)),
        ],
        compiler_params=pltpu.CompilerParams(
            collective_id=0, has_side_effects=True, vmem_limit_bytes=16 * 1024 * 1024
        ),
    )(spacing, field_now, base_cond, source)


def solution(mesh):
    placed = (P("gx", None, "gy"), P("gx", None, "gy"), P("gx"), P("gx", None, "gy"))
    return jax.shard_map(
        functools.partial(per_device, mesh.shape["gx"], mesh.shape["gy"]),
        mesh=mesh,
        in_specs=placed,
        out_specs=(P("gx", None, "gy"), P("gx", None, "gy")),
        check_vma=False,
    )
```

time: 402 us -> 46.2 us (0.11)
  the two profiles are of different devices: /device:TPU:24 before, /device:TPU:32 now
where the time goes in v1:
time: 46.2 us; the launch traced here: 46 us
  Pallas kernels  40.7 us (88%)
  local copies, waits for them, and re-layouts  4.67 us (10%)
  between operations  0.65 us (1%)
    pallas_call x1, Pallas kernels, per_device(): pl.pallas_call(functools.partial(kernel, parts, rows), out_shape=[shape,...  40.7 us
    unnamed x10, local copies, waits for them, and re-layouts  4.67 us

profile of v1, /device:TPU:32, one launch (start us, length us, event | category | flops | bytes accessed | tf_op | source)
XLA Modules:
  0.0 46.0 jit_solution(4864854877302504946)
XLA Ops:
  0.6 0.0 copy-start
  0.6 0.9 %copy-done = f32[32,8,128]{2,1,0:T(8,128)S(1)} copy-done((f32[32,8,128]{2,1,0:T(8,128)S(1)}, f32[32,8,128]{2,1,0:T(8,128)}, u32[]{:S(2)}) %copy-start) | copy-done | bytes 131096
  1.5 0.0 copy-start.1
  1.5 0.9 %copy-done.1 = f32[32,8,128]{2,1,0:T(8,128)S(1)} copy-done((f32[32,8,128]{2,1,0:T(8,128)S(1)}, f32[32,8,128]{2,1,0:T(8,128)}, u32[]{:S(2)}) %copy-start.1) | copy-done | bytes 131096
  2.4 0.0 copy-start.2
  2.4 0.9 %copy-done.2 = f32[32,8,128]{2,1,0:T(8,128)S(1)} copy-done((f32[32,8,128]{2,1,0:T(8,128)S(1)}, f32[32,8,128]{2,1,0:T(8,128)}, u32[]{:S(2)}) %copy-start.2) | copy-done | bytes 131096
  3.3 0.0 copy-start.3
  3.3 0.7 %copy-done.3 = f32[32]{0:T(128)S(1)} copy-done((f32[32]{0:T(128)S(1)}, f32[32]{0:T(128)}, u32[]{:S(2)}) %copy-start.3) | copy-done | bytes 152
  4.0 40.7 %shard_map.59 = (f32[32,8,128]{2,1,0:T(8,128)S(1)}, f32[32,8,128]{2,1,0:T(8,128)S(1)}) custom-call(f32[32]{0:T(128)S(1)} %copy-done.3, f32[32,8,128]{2,1,0:T(8,128)S(1)} %copy-done, f32[32,8,128]{2,1,0:T(8,128)S(1)} %copy-done.1, f32[32,8,128]{2,1,0:T(8,128)S(1)} %copy-done.2), custom_call_target="tpu_custom_call" | custom-call | tf_op jit(solution)/shard_map/pallas_call | solution.py:304
  44.7 0.7 %copy.8 = f32[32,8,128]{2,1,0:T(8,128)} copy(f32[32,8,128]{2,1,0:T(8,128)S(1)} %get-tuple-element.4) | data formatting | bytes 262144
  45.4 0.7 %copy.9 = f32[32,8,128]{2,1,0:T(8,128)} copy(f32[32,8,128]{2,1,0:T(8,128)S(1)} %get-tuple-element.5) | data formatting | bytes 262144
Async XLA Ops:
  0.6 0.9 %copy-start = (f32[32,8,128]{2,1,0:T(8,128)S(1)}, f32[32,8,128]{2,1,0:T(8,128)}, u32[]{:S(2)}) copy-start(f32[32,8,128]{2,1,0:T(8,128)} %f_ref.1) | copy-start | bytes 393220
  1.5 0.9 %copy-start.1 = (f32[32,8,128]{2,1,0:T(8,128)S(1)}, f32[32,8,128]{2,1,0:T(8,128)}, u32[]{:S(2)}) copy-start(f32[32,8,128]{2,1,0:T(8,128)} %k_ref.1) | copy-start | bytes 393220
  2.4 0.9 %copy-start.2 = (f32[32,8,128]{2,1,0:T(8,128)S(1)}, f32[32,8,128]{2,1,0:T(8,128)}, u32[]{:S(2)}) copy-start(f32[32,8,128]{2,1,0:T(8,128)} %s_ref.1) | copy-start | bytes 393220
  3.3 0.7 %copy-start.3 = (f32[32]{0:T(128)S(1)}, f32[32]{0:T(128)}, u32[]{:S(2)}) copy-start(f32[32]{0:T(128)} %h_ref.1) | copy-start | bytes 388

commit v2 on v1

--- a/solution.py
+++ b/solution.py
@@ -22,15 +22,19 @@
 def kernel(
     parts,
     rows,
+    h_hbm,
+    f_hbm,
+    k_hbm,
+    s_hbm,
+    r_ref,
+    rho_ref,
+    width_ref,
+    entry_ref,
     h_ref,
     f_ref,
     k_ref,
     s_ref,
-    u_out,
-    flux_out,
     q_ref,
-    r_ref,
-    rho_ref,
     edge,
     edge_in,
     head,
@@ -39,6 +43,7 @@
     gather,
     state_out,
     state,
+    load,
     y_send,
     y_recv,
     x_send,
@@ -53,42 +58,52 @@
     first_root = FIRST_ROOT % parts
     second_root = SECOND_ROOT % parts
     roots = (first_root, second_root)
-    next_y = lax.rem(gy + 1, rows)
-    prev_y = lax.rem(gy + rows - 1, rows)
-    has_up = gx < parts - 1
-    has_down = gx > 0
+    has_up, has_down = gx < parts - 1, gx > 0
+    has_next, has_prev = gy < rows - 1, gy > 0
 
     barrier = pltpu.get_barrier_semaphore()
 
     def greet(target):
         pl.semaphore_signal(barrier, inc=1, device_id=target, device_id_type=MESH)
 
-    greet({"gy": next_y})
-    greet({"gy": prev_y})
-
-    @pl.when(has_up)
-    def _():
-        greet({"gx": gx + 1})
-
-    @pl.when(has_down)
-    def _():
-        greet({"gx": gx - 1})
+    neighbours = (
+        (has_next, {"gy": gy + 1}),
+        (has_prev, {"gy": gy - 1}),
+        (has_up, {"gx": gx + 1}),
+        (has_down, {"gx": gx - 1}),
+    )
+    greetings = 0
+    for there, target in neighbours:
+        pl.when(there)(functools.partial(greet, target))
+        greetings = greetings + there.astype(jnp.int32)
+
+    loads = [
+        pltpu.make_async_copy(source, target, load.at[i])
+        for i, (source, target) in enumerate(
+            ((f_hbm, f_ref), (k_hbm, k_ref), (s_hbm, s_ref), (h_hbm, h_ref))
+        )
+    ]
+    for copy in loads:
+        copy.start()
+
+    def is_root(root):
+        return gx == root
 
     for root in roots:
-
-        @pl.when(gx == root)
+        greetings = greetings + 1 - is_root(root).astype(jnp.int32)
+
+        @pl.when(is_root(root))
         def _():
             for step in range(1, parts):
                 greet({"gx": lax.rem(gx + step, parts)})
-
-    greetings = 2 + has_up.astype(jnp.int32) + has_down.astype(jnp.int32)
-    for root in roots:
-        greetings = greetings + (gx != root).astype(jnp.int32)
 
     lane = lax.broadcasted_iota(jnp.int32, (8, 128), 1)
     plane = lax.broadcasted_iota(jnp.int32, (8, 128), 0)
     even = lane % 2 == 0
     pair = lane // 2
+
+    loads[0].wait()
+    loads[1].wait()
 
     packed = jnp.zeros((8, 128), jnp.float32)
     for i in range(CELLS):
@@ -98,9 +113,13 @@
         packed = jnp.where(pair == i, pltpu.roll(field, 2 * i + 1, 1), packed)
         packed = jnp.where(pair == i + 32, pltpu.roll(q, (64 + 2 * i + 1) % 128, 1), packed)
     edge[...] = packed
+    loads[3].wait()
+    spacing = h_ref[...]
+    for i in range(CELLS):
+        width_ref[i] = jnp.broadcast_to(spacing[:, i : i + 1], (8, 128))
     head[0] = f_ref[0]
     head[1] = k_ref[0]
-    head[2] = jnp.full((8, 128), h_ref[0], jnp.float32)
+    head[2] = width_ref[0]
 
     pl.semaphore_wait(barrier, greetings)
 
@@ -110,14 +129,13 @@
             dst_ref=edge_in.at[slot],
             send_sem=y_send.at[slot],
             recv_sem=y_recv.at[slot],
-            device_id={"gy": target},
+            device_id={"gy": lax.rem(target + rows, rows)},
             device_id_type=MESH,
         )
 
-    to_next = y_copy(0, next_y)
-    to_prev = y_copy(1, prev_y)
-    to_next.start()
-    to_prev.start()
+    to_next, to_prev = y_copy(0, gy + 1), y_copy(1, gy - 1)
+    pl.when(has_next)(to_next.start)
+    pl.when(has_prev)(to_prev.start)
     to_down = pltpu.make_async_remote_copy(
         src_ref=head,
         dst_ref=head_in,
@@ -130,6 +148,8 @@
     @pl.when(has_down)
     def _():
         to_down.start()
+
+    loads[2].wait()
 
     for i in range(CELLS):
         field, q = f_ref[i], q_ref[i]
@@ -144,7 +164,7 @@
             + s_ref[i]
         )
 
-    h = [h_ref[i] for i in range(CELLS)]
+    h = [width_ref[i] for i in range(CELLS)]
     is_first = gx == 0
     is_last = gx == parts - 1
 
@@ -175,72 +195,84 @@
         for c, value in enumerate((u_a, u_b, f_a, f_b, u_c, f_c)):
             coef[slot, c] = value
 
+    def chain(slot):
+        zero = jnp.zeros((8, 128), jnp.float32)
+        w_u, w_f = zero, zero + 1.0
+        p_u, p_f = zero, zero
+        entries = []
+        for part in range(parts):
+            entries.append((w_u, w_f, p_u, p_f))
+            m11, m12, m21, m22, b_u, b_f = (
+                gather[slot * parts + part, c] for c in range(COEFS)
+            )
+            w_u, w_f = m11 * w_u + m12 * w_f, m21 * w_u + m22 * w_f
+            p_u, p_f = m11 * p_u + m12 * p_f + b_u, m21 * p_u + m22 * p_f + b_f
+        start = -p_u / w_u
+        for part, (w_u, w_f, p_u, p_f) in enumerate(entries):
+            state_out[slot * parts + part, 0] = w_u * start + p_u
+            state_out[slot * parts + part, 1] = w_f * start + p_f
+
     def solve(root, slot):
-        here = gx == root
+        here = is_root(root)
         to_root = pltpu.make_async_remote_copy(
             src_ref=coef.at[slot],
-            dst_ref=gather.at[slot, gx],
+            dst_ref=gather.at[slot * parts + gx],
             send_sem=c_send.at[slot],
             recv_sem=c_recv.at[slot],
             device_id={"gx": root},
             device_id_type=MESH,
         )
-
-        @pl.when(jnp.logical_not(here))
-        def _():
-            to_root.start()
+        pl.when(jnp.logical_not(here))(to_root.start)
 
         @pl.when(here)
         def _():
-            gather[slot, root] = coef[slot]
-            arrived = gather.at[slot, pl.ds(0, parts - 1)]
+            gather[slot * parts + root] = coef[slot]
+            arrived = gather.at[pl.ds(slot * parts, parts - 1)]
             pltpu.make_async_copy(arrived, arrived, c_recv.at[slot]).wait()
-            zero = jnp.zeros((8, 128), jnp.float32)
-            w_u, w_f = zero, zero + 1.0
-            p_u, p_f = zero, zero
-            entries = []
-            for part in range(parts):
-                entries.append((w_u, w_f, p_u, p_f))
-                m11, m12, m21, m22, b_u, b_f = (gather[slot, part, c] for c in range(COEFS))
-                w_u, w_f = m11 * w_u + m12 * w_f, m21 * w_u + m22 * w_f
-                p_u, p_f = m11 * p_u + m12 * p_f + b_u, m21 * p_u + m22 * p_f + b_f
-            start = -p_u / w_u
-            for part, (w_u, w_f, p_u, p_f) in enumerate(entries):
-                state_out[slot, part, 0] = w_u * start + p_u
-                state_out[slot, part, 1] = w_f * start + p_f
+            chain(slot)
             order = sorted(
                 (part for part in range(parts) if part != root),
-                key=lambda part: -min((part - root) % parts, (root - part) % parts),
+                key=lambda part: min((part - root) % parts, (root - part) % parts),
+                reverse=slot == 0,
             )
             for part in order:
                 pltpu.make_async_remote_copy(
-                    src_ref=state_out.at[slot, part],
+                    src_ref=state_out.at[slot * parts + part],
                     dst_ref=state.at[slot],
                     send_sem=s_send.at[slot],
                     recv_sem=s_recv.at[slot],
                     device_id={"gx": part},
                     device_id_type=MESH,
                 ).start()
-            state[slot] = state_out[slot, root]
+            state[slot] = state_out[slot * parts + root]
 
         @pl.when(jnp.logical_not(here))
         def _():
             pltpu.make_async_copy(state.at[slot], state.at[slot], s_recv.at[slot]).wait()
 
     def finish(root, slot):
-        here = gx == root
+        here = is_root(root)
 
         @pl.when(here)
         def _():
-            sent = state_out.at[slot, pl.ds(0, parts - 1)]
+            sent = state_out.at[pl.ds(slot * parts, parts - 1)]
             pltpu.make_async_copy(sent, sent, s_send.at[slot]).wait()
 
         @pl.when(jnp.logical_not(here))
         def _():
             pltpu.make_async_copy(coef.at[slot], coef.at[slot], c_send.at[slot]).wait()
 
-    to_next.wait_recv()
-    to_prev.wait_recv()
+    pl.when(has_prev)(to_next.wait_recv)
+    pl.when(has_next)(to_prev.wait_recv)
+
+    @pl.when(jnp.logical_not(has_prev))
+    def _():
+        edge_in[0] = packed
+
+    @pl.when(jnp.logical_not(has_next))
+    def _():
+        edge_in[1] = packed
+
     own = pltpu.roll(packed, 127, 1)
     other = jnp.where(even, edge_in[0], pltpu.roll(edge_in[1], 126, 1))
     own_q = pltpu.roll(own, 64, 1)
@@ -278,35 +310,40 @@
     transfer(rho_start, 1)
     solve(second_root, 1)
 
-    u, flux = state[1, 0], state[1, 1]
-    u = u - rho_start * flux
-    for i in range(CELLS):
-        flux = flux + (r_ref[i] - h[i] * u)
+    entry_ref[0] = state[1, 0] - rho_start * state[1, 1]
+    entry_ref[1] = state[1, 1]
+    pl.when(has_next)(to_next.wait_send)
+    pl.when(has_prev)(to_prev.wait_send)
+
+    @pl.when(has_down)
+    def _():
+        to_down.wait_send()
+
+    finish(first_root, 0)
+    finish(second_root, 1)
+
+
+def sweep(r_ref, rho_ref, width_ref, entry_ref, u_out, flux_out):
+    u, flux = entry_ref[0], entry_ref[1]
+    for i in range(CELLS):
+        flux = flux + (r_ref[i] - width_ref[i] * u)
         u_out[i] = u
         flux_out[i] = flux * (1.0 / CELLS)
         u = u - rho_ref[i] * flux
 
-    to_next.wait_send()
-    to_prev.wait_send()
-
-    @pl.when(has_down)
-    def _():
-        to_down.wait_send()
-
-    finish(first_root, 0)
-    finish(second_root, 1)
-
 
 def per_device(parts, rows, field_now, base_cond, spacing, source):
-    whole = pl.BlockSpec(memory_space=pltpu.VMEM)
+    vmem = pl.BlockSpec(memory_space=pltpu.VMEM)
     tile = (8, 128)
-    shape = jax.ShapeDtypeStruct(field_now.shape, jnp.float32)
-    return pl.pallas_call(
+    block = jax.ShapeDtypeStruct((CELLS, *tile), jnp.float32)
+    parts_of_system = pl.pallas_call(
         functools.partial(kernel, parts, rows),
-        out_shape=[shape, shape],
-        in_specs=[pl.BlockSpec(memory_space=pltpu.SMEM), whole, whole, whole],
-        out_specs=[whole, whole],
+        out_shape=[pltpu.VMEM((n, *tile), jnp.float32) for n in (CELLS, CELLS, CELLS, 2)],
+        in_specs=[pl.BlockSpec(memory_space=pltpu.HBM)] * 4,
+        out_specs=[vmem] * 4,
         scratch_shapes=[
+            pltpu.VMEM((1, CELLS), jnp.float32),
+            pltpu.VMEM((CELLS, *tile), jnp.float32),
             pltpu.VMEM((CELLS, *tile), jnp.float32),
             pltpu.VMEM((CELLS, *tile), jnp.float32),
             pltpu.VMEM((CELLS, *tile), jnp.float32),
@@ -315,9 +352,10 @@
             pltpu.VMEM((3, *tile), jnp.float32),
             pltpu.VMEM((3, *tile), jnp.float32),
             pltpu.VMEM((2, COEFS, *tile), jnp.float32),
-            pltpu.VMEM((2, parts, COEFS, *tile), jnp.float32),
-            pltpu.VMEM((2, parts, 2, *tile), jnp.float32),
+            pltpu.VMEM((2 * parts, COEFS, *tile), jnp.float32),
+            pltpu.VMEM((2 * parts, 2, *tile), jnp.float32),
             pltpu.VMEM((2, 2, *tile), jnp.float32),
+            pltpu.SemaphoreType.DMA((4,)),
             pltpu.SemaphoreType.DMA((2,)),
             pltpu.SemaphoreType.DMA((2,)),
             pltpu.SemaphoreType.DMA,
@@ -328,9 +366,16 @@
             pltpu.SemaphoreType.DMA((2,)),
         ],
         compiler_params=pltpu.CompilerParams(
-            collective_id=0, has_side_effects=True, vmem_limit_bytes=16 * 1024 * 1024
+            collective_id=0, has_side_effects=True, vmem_limit_bytes=60 * 1024 * 1024
         ),
-    )(spacing, field_now, base_cond, source)
+    )(spacing.reshape(1, CELLS), field_now, base_cond, source)
+    return pl.pallas_call(
+        sweep,
+        out_shape=[block, block],
+        in_specs=[vmem] * 4,
+        out_specs=[vmem] * 2,
+        compiler_params=pltpu.CompilerParams(vmem_limit_bytes=4 * 1024 * 1024),
+    )(*parts_of_system)
 
 
 def solution(mesh):

time: 46.2 us -> 39 us (0.84)
  the two profiles are of different devices: /device:TPU:32 before, /device:TPU:24 now
where the time goes in v2:
time: 39 us; the launch traced here: 38.8 us
  Pallas kernels  38.2 us (98%)
  between operations  0.64 us (2%)
    pallas_call x1, Pallas kernels, per_device(): pl.pallas_call(functools.partial(kernel, parts, rows), out_shape=[pltpu.V...  37.3 us
    pallas_call x1, Pallas kernels, per_device(): pl.pallas_call(sweep, out_shape=[block, block], in_specs=[vmem] * 4, out_...  0.87 us

profile of v2, /device:TPU:24, one launch (start us, length us, event | category | flops | bytes accessed | tf_op | source)
XLA Modules:
  0.0 38.8 jit_solution(14410947801451929609)
XLA Ops:
  0.6 37.3 %shard_map.59 = (f32[32,8,128]{2,1,0:T(8,128)S(1)}, f32[32,8,128]{2,1,0:T(8,128)S(1)}, f32[32,8,128]{2,1,0:T(8,128)S(1)}, f32[2,8,128]{2,1,0:T(8,128)S(1)}) custom-call(f32[1,32]{1,0:T(1,128)} %bitcast.1, f32[32,8,128]{2,1,0:T(8,128)} %f_hbm.1, f32[32,8,128]{2,1,0:T(8,128)} %k_hbm.1, f32[32,8,128]{2,1,0:T(8,128)} %s_hbm.1), custom_call_target="tpu_custom_call" | custom-call | tf_op jit(solution)/shard_map/pallas_call | solution.py:339
  38.0 0.9 %shard_map.60 = (f32[32,8,128]{2,1,0:T(8,128)}, f32[32,8,128]{2,1,0:T(8,128)}) custom-call(f32[32,8,128]{2,1,0:T(8,128)S(1)} %get-tuple-element.6.r_ref, f32[32,8,128]{2,1,0:T(8,128)S(1)} %get-tuple-element.7.rho_ref, f32[32,8,128]{2,1,0:T(8,128)S(1)} %get-tuple-element.8.width_ref, f32[2,8,128]{2,1,0:T(8,128)S(1)} %get-tuple-element.9.entry_ref), custom_call_target="tpu_custom_call" | custom-call | tf_op jit(solution)/shard_map/pallas_call | solution.py:372

commit v3 on v2

--- a/solution.py
+++ b/solution.py
@@ -10,7 +10,7 @@
 MESH = pl.DeviceIdType.MESH
 CELLS = 32
 COEFS = 6
-FIRST_ROOT = 5
+FIRST_ROOT = 4
 SECOND_ROOT = 0
 
 
@@ -58,6 +58,7 @@
     first_root = FIRST_ROOT % parts
     second_root = SECOND_ROOT % parts
     roots = (first_root, second_root)
+    other_y = jnp.where(gy % 2 == 0, gy + 1, gy - 1)
     has_up, has_down = gx < parts - 1, gx > 0
     has_next, has_prev = gy < rows - 1, gy > 0
 
@@ -90,12 +91,12 @@
         return gx == root
 
     for root in roots:
-        greetings = greetings + 1 - is_root(root).astype(jnp.int32)
+        greetings = greetings + 1
 
         @pl.when(is_root(root))
         def _():
-            for step in range(1, parts):
-                greet({"gx": lax.rem(gx + step, parts)})
+            for step in range(parts):
+                greet({"gx": lax.rem(gx + step, parts), "gy": other_y})
 
     lane = lax.broadcasted_iota(jnp.int32, (8, 128), 1)
     plane = lax.broadcasted_iota(jnp.int32, (8, 128), 0)
@@ -219,19 +220,18 @@
             dst_ref=gather.at[slot * parts + gx],
             send_sem=c_send.at[slot],
             recv_sem=c_recv.at[slot],
-            device_id={"gx": root},
+            device_id={"gx": root, "gy": other_y},
             device_id_type=MESH,
         )
-        pl.when(jnp.logical_not(here))(to_root.start)
+        to_root.start()
 
         @pl.when(here)
         def _():
-            gather[slot * parts + root] = coef[slot]
-            arrived = gather.at[pl.ds(slot * parts, parts - 1)]
+            arrived = gather.at[pl.ds(slot * parts, parts)]
             pltpu.make_async_copy(arrived, arrived, c_recv.at[slot]).wait()
             chain(slot)
             order = sorted(
-                (part for part in range(parts) if part != root),
+                range(parts),
                 key=lambda part: min((part - root) % parts, (root - part) % parts),
                 reverse=slot == 0,
             )
@@ -241,24 +241,21 @@
                     dst_ref=state.at[slot],
                     send_sem=s_send.at[slot],
                     recv_sem=s_recv.at[slot],
-                    device_id={"gx": part},
+                    device_id={"gx": part, "gy": other_y},
                     device_id_type=MESH,
                 ).start()
-            state[slot] = state_out[slot * parts + root]
-
-        @pl.when(jnp.logical_not(here))
-        def _():
-            pltpu.make_async_copy(state.at[slot], state.at[slot], s_recv.at[slot]).wait()
+
+        pltpu.make_async_copy(state.at[slot], state.at[slot], s_recv.at[slot]).wait()
 
     def finish(root, slot):
         here = is_root(root)
 
         @pl.when(here)
         def _():
-            sent = state_out.at[pl.ds(slot * parts, parts - 1)]
+            sent = state_out.at[pl.ds(slot * parts, parts)]
             pltpu.make_async_copy(sent, sent, s_send.at[slot]).wait()
 
-        @pl.when(jnp.logical_not(here))
+        @pl.when(gx >= 0)
         def _():
             pltpu.make_async_copy(coef.at[slot], coef.at[slot], c_send.at[slot]).wait()
 

time: 39 us -> 38.4 us (0.985)
  Pallas kernels: 38.2 us -> 37.4 us
    pallas_call x1, Pallas kernels: 37.3 us -> 36.6 us  [per_device(): pl.pallas_call(functools.partial(kernel, parts, rows), out_shape=[pltpu.V...]
where the time goes in v3:
time: 38.4 us; the launch traced here: 38.1 us
  Pallas kernels  37.4 us (97%)
  between operations  0.64 us (2%)
    pallas_call x1, Pallas kernels, per_device(): pl.pallas_call(functools.partial(kernel, parts, rows), out_shape=[pltpu.V...  36.6 us
    pallas_call x1, Pallas kernels, per_device(): pl.pallas_call(sweep, out_shape=[block, block], in_specs=[vmem] * 4, out_...  0.87 us

profile of v3, /device:TPU:24, one launch (start us, length us, event | category | flops | bytes accessed | tf_op | source)
XLA Modules:
  0.0 38.1 jit_solution(14410283835518436946)
XLA Ops:
  0.6 36.6 %shard_map.59 = (f32[32,8,128]{2,1,0:T(8,128)S(1)}, f32[32,8,128]{2,1,0:T(8,128)S(1)}, f32[32,8,128]{2,1,0:T(8,128)S(1)}, f32[2,8,128]{2,1,0:T(8,128)S(1)}) custom-call(f32[1,32]{1,0:T(1,128)} %bitcast.1, f32[32,8,128]{2,1,0:T(8,128)} %f_hbm.1, f32[32,8,128]{2,1,0:T(8,128)} %k_hbm.1, f32[32,8,128]{2,1,0:T(8,128)} %s_hbm.1), custom_call_target="tpu_custom_call" | custom-call | tf_op jit(solution)/shard_map/pallas_call | solution.py:336
  37.2 0.9 %shard_map.60 = (f32[32,8,128]{2,1,0:T(8,128)}, f32[32,8,128]{2,1,0:T(8,128)}) custom-call(f32[32,8,128]{2,1,0:T(8,128)S(1)} %get-tuple-element.6.r_ref, f32[32,8,128]{2,1,0:T(8,128)S(1)} %get-tuple-element.7.rho_ref, f32[32,8,128]{2,1,0:T(8,128)S(1)} %get-tuple-element.8.width_ref, f32[2,8,128]{2,1,0:T(8,128)S(1)} %get-tuple-element.9.entry_ref), custom_call_target="tpu_custom_call" | custom-call | tf_op jit(solution)/shard_map/pallas_call | solution.py:369

commit v4 on v3

v4 whole, which is shorter than its diff:
```python
import functools

import jax
import jax.numpy as jnp
from jax import lax
from jax.experimental import pallas as pl
from jax.experimental.pallas import tpu as pltpu
from jax.sharding import PartitionSpec as P

MESH = pl.DeviceIdType.MESH
CELLS = 32
LAST = CELLS - 1
SCALE = 1.0 / (16.0 * CELLS * CELLS)
FIRST_ROOT = 4
SECOND_ROOT = 0


def resistivity(field, base_cond):
    square = field * field
    return (1.0 + square) / (base_cond * (1.0 + 2.0 * square))


def kernel(
    parts,
    rows,
    h_hbm,
    f_hbm,
    k_hbm,
    s_hbm,
    r_ref,
    rho_ref,
    width_ref,
    entry_ref,
    h_ref,
    f_ref,
    k_ref,
    s_ref,
    q_ref,
    edge,
    edge_in,
    head,
    head_in,
    matrix,
    vector,
    coef,
    matrices,
    vectors,
    coefs,
    corner_ref,
    answer,
    state,
    load,
    send,
    recv,
):
    gx = lax.axis_index("gx")
    gy = lax.axis_index("gy")
    first_root = FIRST_ROOT % parts
    second_root = SECOND_ROOT % parts
    is_even = gy % 2 == 0
    other_y = jnp.where(is_even, gy + 1, gy - 1)
    has_up, has_down = gx < parts - 1, gx > 0
    has_next, has_prev = gy < rows - 1, gy > 0
    first_here, second_here = gx == first_root, gx == second_root

    barrier = pltpu.get_barrier_semaphore()

    def greet(target):
        pl.semaphore_signal(barrier, inc=1, device_id=target, device_id_type=MESH)

    neighbours = (
        (has_next, {"gy": gy + 1}),
        (has_prev, {"gy": gy - 1}),
        (has_up, {"gx": gx + 1}),
        (has_down, {"gx": gx - 1}),
    )
    greetings = 2
    for there, target in neighbours:
        pl.when(there)(functools.partial(greet, target))
        greetings = greetings + there.astype(jnp.int32)

    loads = [
        pltpu.make_async_copy(source, target, load.at[i])
        for i, (source, target) in enumerate(
            ((f_hbm, f_ref), (k_hbm, k_ref), (s_hbm, s_ref), (h_hbm, h_ref))
        )
    ]
    for copy in loads:
        copy.start()

    for here in (first_here, second_here):

        @pl.when(here)
        def _():
            for step in range(parts):
                greet({"gx": lax.rem(gx + step, parts), "gy": other_y})

    lane = lax.broadcasted_iota(jnp.int32, (8, 128), 1)
    plane = lax.broadcasted_iota(jnp.int32, (8, 128), 0)
    even = lane % 2 == 0
    pair = lane // 2
    rim_pair = ((lane + 1) % 128) // 2
    rim = jnp.logical_or(lane == 0, lane == 127)

    loads[0].wait()
    loads[1].wait()

    packed = jnp.zeros((8, 128), jnp.float32)
    for i in range(CELLS):
        field = f_ref[i]
        q = resistivity(field, k_ref[i])
        q_ref[i] = q
        packed = jnp.where(pair == i, pltpu.roll(field, 2 * i + 1, 1), packed)
        packed = jnp.where(pair == i + 32, pltpu.roll(q, (64 + 2 * i + 1) % 128, 1), packed)
    loads[3].wait()
    spacing = h_ref[...]
    for i in range(CELLS):
        width_ref[i] = jnp.broadcast_to(spacing[:, i : i + 1], (8, 128))
    edge[...] = packed
    head[0] = f_ref[0]
    head[1] = k_ref[0]
    head[2] = width_ref[0]

    pl.semaphore_wait(barrier, greetings)

    def remote(index, source, target, **device):
        return pltpu.make_async_remote_copy(
            src_ref=source,
            dst_ref=target,
            send_sem=send.at[index],
            recv_sem=recv.at[index],
            device_id=device,
            device_id_type=MESH,
        )

    def wait_for(ref, semaphore):
        pltpu.make_async_copy(ref, ref, semaphore).wait()

    to_next = remote(0, edge, edge_in.at[0], gy=lax.rem(gy + 1, rows))
    to_prev = remote(1, edge, edge_in.at[1], gy=lax.rem(gy + rows - 1, rows))
    to_down = remote(2, head, head_in, gx=lax.rem(gx + parts - 1, parts))
    pl.when(has_next)(to_next.start)
    pl.when(has_prev)(to_prev.start)
    pl.when(has_down)(to_down.start)

    loads[2].wait()
    for i in range(CELLS):
        field, q = f_ref[i], q_ref[i]
        face_y = 0.3 / (q + pltpu.roll(q, 127, 1)) * (pltpu.roll(field, 127, 1) - field)
        face_y = jnp.where(lane == 127, 0.0, face_y)
        face_z = 0.2 / (q + pltpu.roll(q, 7, 0)) * (pltpu.roll(field, 7, 0) - field)
        face_z = jnp.where(plane == 7, 0.0, face_z)
        r_ref[i] = width_ref[i] * (
            field
            + (face_y - pltpu.roll(face_y, 1, 1))
            + (face_z - pltpu.roll(face_z, 1, 0))
            + s_ref[i]
        )

    def reduce_segment(weights):
        zero = jnp.zeros((8, 128), jnp.float32)
        packed_weights = zero
        s_u, s_f = zero + 1.0, zero
        p_u, p_f = zero, zero + 1.0
        b_u, b_f = zero, zero
        for i in reversed(range(CELLS)):
            h = width_ref[i]
            if i < LAST:
                rho = ((h + width_ref[i + 1]) * SCALE) * (q_ref[i] + q_ref[i + 1])
                rho_ref[i] = rho
                p_u = p_u - rho * s_u
                p_f = p_f - rho * s_f
            b_u = b_u + p_u * r_ref[i]
            b_f = b_f + p_f * r_ref[i]
            h_u, h_f = h * p_u, h * p_f
            s_u = s_u - h_u
            s_f = s_f - h_f
            if weights:
                packed_weights = jnp.where(
                    rim_pair == i, pltpu.roll(h_u, 2 * i, 1), packed_weights
                )
                packed_weights = jnp.where(
                    rim_pair == i + 32, pltpu.roll(h_f, 64 + 2 * i, 1), packed_weights
                )
        rho_start = jnp.where(gx == 0, (4.0 * SCALE) * width_ref[0] * q_ref[0], 0.0)
        p_u, p_f = p_u - rho_start * s_u, p_f - rho_start * s_f
        return rho_start, (s_u, p_u, s_f, p_f), (b_u, b_f), packed_weights

    def last_face(q_next):
        q_last, h_last = q_ref[LAST], width_ref[LAST]
        q_next = jnp.where(has_up, q_next, q_last)
        h_next = jnp.where(has_up, head_in[2], h_last)
        return ((h_last + h_next) * SCALE) * (q_last + q_next)

    def corner(m11, m12, m21):
        return (1.0 + m12 * m21) / m11

    def chain(slot, rows_of):
        zero = jnp.zeros((8, 128), jnp.float32)
        w_u, w_f = zero, zero + 1.0
        p_u, p_f = zero, zero
        entries = []
        for part in range(parts):
            entries.append((w_u, w_f, p_u, p_f))
            m11, m12, m21, m22, b_u, b_f, rho = rows_of(part)
            w_u, w_f = m11 * w_u + m12 * w_f, m21 * w_u + m22 * w_f
            p_u, p_f = m11 * p_u + m12 * p_f + b_u, m21 * p_u + m22 * p_f + b_f
            if rho is not None:
                w_u, p_u = w_u - rho * w_f, p_u - rho * p_f
        start = -p_u / w_u
        for part, (w_u, w_f, p_u, p_f) in enumerate(entries):
            answer[slot * parts + part, 0] = w_u * start + p_u
            answer[slot * parts + part, 1] = w_f * start + p_f

    def give_back(slot, index, root):
        order = sorted(
            range(parts),
            key=lambda part: min((part - root) % parts, (root - part) % parts),
            reverse=slot == 0,
        )
        for part in order:
            source = answer.at[slot * parts + part]
            remote(index, source, state.at[slot], gx=part, gy=other_y).start()

    rho_start, values, (b_u, b_f), packed_weights = reduce_segment(True)
    for c in range(3):
        matrix[c] = values[c]
    remote(3, matrix, matrices.at[gx], gx=first_root, gy=other_y).start()

    pl.when(has_prev)(to_next.wait_recv)
    pl.when(has_next)(to_prev.wait_recv)

    @pl.when(jnp.logical_not(has_prev))
    def _():
        edge_in[0] = packed

    @pl.when(jnp.logical_not(has_next))
    def _():
        edge_in[1] = packed

    own = pltpu.roll(packed, 127, 1)
    other = jnp.where(even, edge_in[0], pltpu.roll(edge_in[1], 126, 1))
    own_q = pltpu.roll(own, 64, 1)
    other_q = pltpu.roll(other, 64, 1)
    outside = jnp.logical_or(
        jnp.logical_and(even, gy == 0),
        jnp.logical_and(jnp.logical_not(even), gy == rows - 1),
    )
    faces = jnp.where(outside, 0.0, 0.3 / (own_q + other_q) * (other - own))
    faces = jnp.where(rim_pair < 32, faces, 0.0)
    total = (faces + pltpu.roll(faces, 64, 1)) * packed_weights
    for shift in (2, 4, 8, 16, 32):
        total = total + pltpu.roll(total, 128 - shift, 1)
    vector[0] = b_u + jnp.where(rim, total, 0.0)
    vector[1] = b_f + jnp.where(rim, pltpu.roll(total, 64, 1), 0.0)

    pl.when(has_up)(to_down.wait_recv)

    @pl.when(jnp.logical_not(has_up))
    def _():
        head_in[...] = jnp.ones_like(head_in)

    last_rho = last_face(resistivity(head_in[0], head_in[1]))
    vector[2] = last_rho
    remote(4, vector, vectors.at[gx], gx=first_root, gy=other_y).start()

    for i in range(CELLS):
        extra = jnp.where(rim, pltpu.roll(faces, (128 - 2 * i) % 128, 1), 0.0)
        r_ref[i] = r_ref[i] + width_ref[i] * extra

    @pl.when(first_here)
    def _():
        wait_for(matrices, recv.at[3])
        corners = [corner(*(matrices[part, c] for c in range(3))) for part in range(parts)]
        for part in range(parts):
            corner_ref[part] = corners[part]
        wait_for(vectors, recv.at[4])

        def rows_of(part):
            m = tuple(matrices[part, c] for c in range(3))
            return (*m, corner_ref[part], *(vectors[part, c] for c in range(3)))

        chain(0, rows_of)
        give_back(0, 5, first_root)

    wait_for(state.at[0], recv.at[5])

    u, flux = state[0, 0], state[0, 1]
    u = u - rho_start * flux
    for i in range(CELLS):
        flux = flux + (r_ref[i] - width_ref[i] * u)
        q_ref[i] = resistivity(0.5 * (f_ref[i] + u), k_ref[i])
        u = u - (rho_ref[i] if i < LAST else last_rho) * flux

    last_rho = last_face(resistivity(0.5 * (head_in[0] + u), head_in[1]))
    rho_start, (m11, m12, m21, m22), (b_u, b_f), _ = reduce_segment(False)
    values = (m11 - last_rho * m21, m12 - last_rho * m22, m21, b_u - last_rho * b_f, b_f)
    for c, value in enumerate(values):
        coef[c] = value
    remote(6, coef, coefs.at[gx], gx=second_root, gy=other_y).start()

    @pl.when(second_here)
    def _():
        wait_for(coefs, recv.at[6])

        def rows_of(part):
            m11, m12, m21, b_u, b_f = (coefs[part, c] for c in range(5))
            return m11, m12, m21, corner(m11, m12, m21), b_u, b_f, None

        chain(1, rows_of)
        give_back(1, 7, second_root)

    wait_for(state.at[1], recv.at[7])
    entry_ref[0] = state[1, 0] - rho_start * state[1, 1]
    entry_ref[1] = state[1, 1]

    pl.when(has_next)(to_next.wait_send)
    pl.when(has_prev)(to_prev.wait_send)
    pl.when(has_down)(to_down.wait_send)
    wait_for(matrix, send.at[3])
    wait_for(vector, send.at[4])
    wait_for(coef, send.at[6])

    @pl.when(first_here)
    def _():
        wait_for(answer.at[pl.ds(0, parts)], send.at[5])

    @pl.when(second_here)
    def _():
        wait_for(answer.at[pl.ds(parts, parts)], send.at[7])


def sweep(r_ref, rho_ref, width_ref, entry_ref, u_out, flux_out):
    u, flux = entry_ref[0], entry_ref[1]
    for i in range(CELLS):
        flux = flux + (r_ref[i] - width_ref[i] * u)
        u_out[i] = u
        flux_out[i] = flux * (1.0 / CELLS)
        if i < LAST:
            u = u - rho_ref[i] * flux


def per_device(parts, rows, field_now, base_cond, spacing, source):
    vmem = pl.BlockSpec(memory_space=pltpu.VMEM)
    block = jax.ShapeDtypeStruct((CELLS, 8, 128), jnp.float32)

    def tiles(*count):
        return pltpu.VMEM((*count, 8, 128), jnp.float32)

    system = pl.pallas_call(
        functools.partial(kernel, parts, rows),
        out_shape=[tiles(CELLS), tiles(CELLS), tiles(CELLS), tiles(2)],
        in_specs=[pl.BlockSpec(memory_space=pltpu.HBM)] * 4,
        out_specs=[vmem] * 4,
        scratch_shapes=[
            pltpu.VMEM((1, CELLS), jnp.float32),
            tiles(CELLS),
            tiles(CELLS),
            tiles(CELLS),
            tiles(CELLS),
            pltpu.VMEM((8, 128), jnp.float32),
            tiles(2),
            tiles(3),
            tiles(3),
            tiles(3),
            tiles(3),
            tiles(5),
            tiles(parts, 3),
            tiles(parts, 3),
            tiles(parts, 5),
            tiles(parts),
            tiles(2 * parts, 2),
            tiles(2, 2),
            pltpu.SemaphoreType.DMA((4,)),
            pltpu.SemaphoreType.DMA((8,)),
            pltpu.SemaphoreType.DMA((8,)),
        ],
        compiler_params=pltpu.CompilerParams(
            collective_id=0, has_side_effects=True, vmem_limit_bytes=60 * 1024 * 1024
        ),
    )(spacing.reshape(1, CELLS), field_now, base_cond, source)
    return pl.pallas_call(
        sweep,
        out_shape=[block, block],
        in_specs=[vmem] * 4,
        out_specs=[vmem] * 2,
        compiler_params=pltpu.CompilerParams(vmem_limit_bytes=4 * 1024 * 1024),
    )(*system)


def solution(mesh):
    placed = (P("gx", None, "gy"), P("gx", None, "gy"), P("gx"), P("gx", None, "gy"))
    return jax.shard_map(
        functools.partial(per_device, mesh.shape["gx"], mesh.shape["gy"]),
        mesh=mesh,
        in_specs=placed,
        out_specs=(P("gx", None, "gy"), P("gx", None, "gy")),
        check_vma=False,
    )
```

time: 38.4 us -> 38.1 us (level)
  the two profiles are of different devices: /device:TPU:24 before, /device:TPU:17 now
where the time goes in v4:
time: 38.1 us; the launch traced here: 38 us
  Pallas kernels  37.3 us (98%)
  between operations  0.64 us (2%)
    pallas_call x1, Pallas kernels, per_device(): pl.pallas_call(functools.partial(kernel, parts, rows), out_shape=[tiles(C...  36.5 us
    pallas_call x1, Pallas kernels, per_device(): pl.pallas_call(sweep, out_shape=[block, block], in_specs=[vmem] * 4, out_...  0.87 us

profile of v4, /device:TPU:17, one launch (start us, length us, event | category | flops | bytes accessed | tf_op | source)
XLA Modules:
  0.0 38.0 jit_solution(1919721413811507115)
XLA Ops:
  0.6 36.5 %shard_map.59 = (f32[32,8,128]{2,1,0:T(8,128)S(1)}, f32[32,8,128]{2,1,0:T(8,128)S(1)}, f32[32,8,128]{2,1,0:T(8,128)S(1)}, f32[2,8,128]{2,1,0:T(8,128)S(1)}) custom-call(f32[1,32]{1,0:T(1,128)} %bitcast.1, f32[32,8,128]{2,1,0:T(8,128)} %f_hbm.1, f32[32,8,128]{2,1,0:T(8,128)} %k_hbm.1, f32[32,8,128]{2,1,0:T(8,128)} %s_hbm.1), custom_call_target="tpu_custom_call" | custom-call | tf_op jit(solution)/shard_map/pallas_call | solution.py:350
  37.1 0.9 %shard_map.60 = (f32[32,8,128]{2,1,0:T(8,128)}, f32[32,8,128]{2,1,0:T(8,128)}) custom-call(f32[32,8,128]{2,1,0:T(8,128)S(1)} %get-tuple-element.6.r_ref, f32[32,8,128]{2,1,0:T(8,128)S(1)} %get-tuple-element.7.rho_ref, f32[32,8,128]{2,1,0:T(8,128)S(1)} %get-tuple-element.8.width_ref, f32[2,8,128]{2,1,0:T(8,128)S(1)} %get-tuple-element.9.entry_ref), custom_call_target="tpu_custom_call" | custom-call | tf_op jit(solution)/shard_map/pallas_call | solution.py:382

commit v5 on v4

--- a/solution.py
+++ b/solution.py
@@ -27,10 +27,11 @@
     f_hbm,
     k_hbm,
     s_hbm,
+    modes_ref,
+    entry_ref,
     r_ref,
     rho_ref,
     width_ref,
-    entry_ref,
     h_ref,
     f_ref,
     k_ref,
@@ -186,6 +187,24 @@
         p_u, p_f = p_u - rho_start * s_u, p_f - rho_start * s_f
         return rho_start, (s_u, p_u, s_f, p_f), (b_u, b_f), packed_weights
 
+    def propagate(rho_start, last_rho, keep):
+        zero = jnp.zeros((8, 128), jnp.float32)
+        u_a, f_a = zero + 1.0, zero
+        u_b, f_b = zero - rho_start, zero + 1.0
+        u_c, f_c = zero, zero
+        for i in range(CELLS):
+            h, rho = width_ref[i], rho_ref[i] if i < LAST else last_rho
+            f_a = f_a - h * u_a
+            f_b = f_b - h * u_b
+            f_c = f_c + (r_ref[i] - h * u_c)
+            for c, value in enumerate((u_a, u_b, u_c, f_a, f_b, f_c)):
+                if c < 3 or keep:
+                    modes_ref[i, c] = value
+            u_a = u_a - rho * f_a
+            u_b = u_b - rho * f_b
+            u_c = u_c - rho * f_c
+        return u_a, u_b, u_c
+
     def last_face(q_next):
         q_last, h_last = q_ref[LAST], width_ref[LAST]
         q_next = jnp.where(has_up, q_next, q_last)
@@ -283,14 +302,14 @@
         chain(0, rows_of)
         give_back(0, 5, first_root)
 
+    u_a, u_b, u_c = propagate(rho_start, last_rho, False)
     wait_for(state.at[0], recv.at[5])
 
-    u, flux = state[0, 0], state[0, 1]
-    u = u - rho_start * flux
-    for i in range(CELLS):
-        flux = flux + (r_ref[i] - width_ref[i] * u)
+    u_in, f_in = state[0, 0], state[0, 1]
+    for i in range(CELLS):
+        u = modes_ref[i, 0] * u_in + modes_ref[i, 1] * f_in + modes_ref[i, 2]
         q_ref[i] = resistivity(0.5 * (f_ref[i] + u), k_ref[i])
-        u = u - (rho_ref[i] if i < LAST else last_rho) * flux
+    u = u_a * u_in + u_b * f_in + u_c
 
     last_rho = last_face(resistivity(0.5 * (head_in[0] + u), head_in[1]))
     rho_start, (m11, m12, m21, m22), (b_u, b_f), _ = reduce_segment(False)
@@ -310,9 +329,9 @@
         chain(1, rows_of)
         give_back(1, 7, second_root)
 
+    propagate(rho_start, last_rho, True)
     wait_for(state.at[1], recv.at[7])
-    entry_ref[0] = state[1, 0] - rho_start * state[1, 1]
-    entry_ref[1] = state[1, 1]
+    entry_ref[...] = state[1]
 
     pl.when(has_next)(to_next.wait_send)
     pl.when(has_prev)(to_prev.wait_send)
@@ -330,14 +349,12 @@
         wait_for(answer.at[pl.ds(parts, parts)], send.at[7])
 
 
-def sweep(r_ref, rho_ref, width_ref, entry_ref, u_out, flux_out):
+def combine(modes_ref, entry_ref, u_out, flux_out):
     u, flux = entry_ref[0], entry_ref[1]
     for i in range(CELLS):
-        flux = flux + (r_ref[i] - width_ref[i] * u)
-        u_out[i] = u
-        flux_out[i] = flux * (1.0 / CELLS)
-        if i < LAST:
-            u = u - rho_ref[i] * flux
+        u_a, u_b, u_c, f_a, f_b, f_c = (modes_ref[i, c] for c in range(6))
+        u_out[i] = u_a * u + u_b * flux + u_c
+        flux_out[i] = (f_a * u + f_b * flux + f_c) * (1.0 / CELLS)
 
 
 def per_device(parts, rows, field_now, base_cond, spacing, source):
@@ -349,10 +366,13 @@
 
     system = pl.pallas_call(
         functools.partial(kernel, parts, rows),
-        out_shape=[tiles(CELLS), tiles(CELLS), tiles(CELLS), tiles(2)],
+        out_shape=[tiles(CELLS, 6), tiles(2)],
         in_specs=[pl.BlockSpec(memory_space=pltpu.HBM)] * 4,
-        out_specs=[vmem] * 4,
+        out_specs=[vmem] * 2,
         scratch_shapes=[
+            tiles(CELLS),
+            tiles(CELLS),
+            tiles(CELLS),
             pltpu.VMEM((1, CELLS), jnp.float32),
             tiles(CELLS),
             tiles(CELLS),
@@ -380,9 +400,9 @@
         ),
     )(spacing.reshape(1, CELLS), field_now, base_cond, source)
     return pl.pallas_call(
-        sweep,
+        combine,
         out_shape=[block, block],
-        in_specs=[vmem] * 4,
+        in_specs=[vmem] * 2,
         out_specs=[vmem] * 2,
         compiler_params=pltpu.CompilerParams(vmem_limit_bytes=4 * 1024 * 1024),
     )(*system)

time: 38.1 us -> 37.9 us (level)
  no operation moved by 1% of the time
where the time goes in v5:
time: 37.9 us; the launch traced here: 37.7 us
  Pallas kernels  37.1 us (98%)
  between operations  0.64 us (2%)
    pallas_call x1, Pallas kernels, per_device(): pl.pallas_call(functools.partial(kernel, parts, rows), out_shape=[tiles(C...  36.3 us

profile of v5, /device:TPU:17, one launch (start us, length us, event | category | flops | bytes accessed | tf_op | source)
XLA Modules:
  0.0 37.7 jit_solution(3935444562324700489)
XLA Ops:
  0.6 36.3 %shard_map.59 = (f32[32,6,8,128]{3,2,1,0:T(8,128)S(1)}, f32[2,8,128]{2,1,0:T(8,128)S(1)}) custom-call(f32[1,32]{1,0:T(1,128)} %bitcast.1, f32[32,8,128]{2,1,0:T(8,128)} %f_hbm.1, f32[32,8,128]{2,1,0:T(8,128)} %k_hbm.1, f32[32,8,128]{2,1,0:T(8,128)} %s_hbm.1), custom_call_target="tpu_custom_call" | custom-call | tf_op jit(solution)/shard_map/pallas_call | solution.py:367
  37.0 0.7 %shard_map.60 = (f32[32,8,128]{2,1,0:T(8,128)}, f32[32,8,128]{2,1,0:T(8,128)}) custom-call(f32[32,6,8,128]{3,2,1,0:T(8,128)S(1)} %get-tuple-element.4.modes_ref, f32[2,8,128]{2,1,0:T(8,128)S(1)} %get-tuple-element.5.entry_ref), custom_call_target="tpu_custom_call" | custom-call | tf_op jit(solution)/shard_map/pallas_call | solution.py:402
